TPU v7x, 32 devices: a whole 2x2x4 slice. The times are simulated.
32 devices in a mesh: dp: 8 (over z, y), seq: 4 (over x, core).
Axes of the slice: x: 2, y: 2, z: 4, core: 2. Of those that a mesh axis runs over, the one named last changes fastest.
Arguments:
- frames: bfloat16 [16384, 1024], P(('dp', 'seq')), may hold values from -6 to 6
- cotangent: bfloat16 [16384, 1024], P(('dp', 'seq')), may hold values from -6 to 6
- clip_len: int32 [8, 3], P('dp'), may hold values from 128 to 1792, as said below
- ln1_gain: float32 [1024], replicated, may hold values from 0.5 to 1.5
- ln1_bias: float32 [1024], replicated, may hold values from -1.75 to 1.75
- w_qkv: bfloat16 [1024, 3072], replicated, may hold values from -0.1875 to 0.1875
- w_out: bfloat16 [1024, 1024], replicated, may hold values from -0.75 to 0.75
- scale_attn: float32 [1024], replicated, may hold values from 0.5 to 1.5
- ln2_gain: float32 [1024], replicated, may hold values from 0.5 to 1.5
- ln2_bias: float32 [1024], replicated, may hold values from -1.75 to 1.75
- w_gate_up: bfloat16 [1024, 8192], replicated, may hold values from -0.1875 to 0.1875
- w_down: bfloat16 [4096, 1024], replicated, may hold values from -0.1875 to 0.1875
- scale_mlp: float32 [1024], replicated, may hold values from 0.5 to 1.5
Outputs:
- out_frames: bfloat16 [16384, 1024], P(('dp', 'seq'))
- input_grad: float32 [16384, 1024], P(('dp', 'seq'))
- grad_ln1_gain: float32 [1024], replicated
- grad_ln1_bias: float32 [1024], replicated
- grad_w_qkv: float32 [1024, 3072], P('dp', 'seq')
- grad_w_out: float32 [1024, 1024], P('dp', 'seq')
- grad_scale_attn: float32 [1024], replicated
- grad_ln2_gain: float32 [1024], replicated
- grad_ln2_bias: float32 [1024], replicated
- grad_w_gate_up: float32 [1024, 8192], P('dp', 'seq')
- grad_w_down: float32 [4096, 1024], P('dp', 'seq')
- grad_scale_mlp: float32 [1024], replicated
Inputs may be any that keep to these rules, and one draw needn't show every extreme that they name: `clip_len`: each group's clips, followed by padding of at most 32 frames, fill its 2048 frames; one clip of each group begins within the group's first 512 frames and ends within its last 512 frames.
All inputs are finite; a program needn't handle non-finite values.
Results may differ from a plain program's by a relative error of at most 0.015.
Values may be sent and summed in bfloat16 or wider, within the bound.
A program may use at most 256 MiB of HBM per device.

v0:
```python
import functools

import jax
import jax.numpy as jnp
import numpy as np
from jax import lax
from jax.experimental import pallas as pl
from jax.experimental.pallas import tpu as pltpu
from jax.sharding import PartitionSpec as P

D = 1024
HEADS = 16
HEAD_DIM = 64
FF = 4096
HALF = 64
QBLK = 512


EPS = 1e-05
NEG = -1e30


def contract_rows(left, right):
    return lax.dot_general(
        left, right, (((0,), (0,)), ((), ())), preferred_element_type=jnp.float32
    )


def contract_back(grads, weight):
    return lax.dot_general(
        grads, weight, (((1,), (1,)), ((), ())), preferred_element_type=jnp.float32
    )


def to_blocks(matrix, data_count, seq_count):
    row_total, col_total = matrix.shape
    shaped = matrix.reshape(data_count, row_total // data_count, seq_count, col_total // seq_count)
    return shaped.transpose(0, 2, 1, 3).reshape(
        data_count * seq_count, row_total // data_count, col_total // seq_count
    )


MESH = pl.DeviceIdType.MESH
TOK = 512
PARTS = (0, 48, 96, 128)

UNITS = (
    [(2, 0, 128, 2, 2048, 256 * v, 2, 0) for v in range(8)]
    + [(3, 128 * v, 512, 3, 256, 0, 3, 128 * v) for v in range(4)]
    + [(1, 0, 128, 1, 256, 0, 1, 0)]
    + [(0, 0, 128, 0, 768, 256 * v, 0, 0) for v in range(3)]
)


def tn_dot(left, right):
    return lax.dot_general(
        left, right, (((0,), (0,)), ((), ())), preferred_element_type=jnp.float32
    )


def rotated(values, cosines, sines):
    lane = lax.broadcasted_iota(jnp.int32, values.shape, 1)
    partner = jnp.where(
        lane % HEAD_DIM < HEAD_DIM // 2,
        pltpu.roll(values, 128 - HEAD_DIM // 2, 1),
        pltpu.roll(values, HEAD_DIM // 2, 1),
    )
    return values * cosines + partner * sines


def head_masks():
    lane = lax.broadcasted_iota(jnp.int32, (128, 128), 1)
    return lane < HEAD_DIM


def stacked(pair):
    first = head_masks()
    zero = jnp.zeros_like(pair)
    return jnp.concatenate([jnp.where(first, pair, zero), jnp.where(first, zero, pair)], 0)


def merged(rows):
    return jnp.where(head_masks(), rows[:128], rows[128:])


def clip_number(positions, ends, group_len):
    total = jnp.zeros_like(positions)
    for end in ends:
        total = total + (positions >= end).astype(jnp.int32)
    return jnp.where((positions >= 0) & (positions < group_len), total, -1)


def normalize(values):
    average = jnp.mean(values, -1, keepdims=True)
    centered = values - average
    inverse = lax.rsqrt(jnp.mean(centered * centered, -1, keepdims=True) + EPS)
    return centered * inverse, inverse


def dot(left, right):
    return jnp.dot(left, right, preferred_element_type=jnp.float32)


def norm_backward(grads, hat, inverse, gain):
    scaled = grads * gain
    return inverse * (
        scaled
        - jnp.mean(scaled, -1, keepdims=True)
        - hat * jnp.mean(scaled * hat, -1, keepdims=True)
    )


def window_bias(bias_ref, clip_ref, group_len, keys_first):
    seq = lax.axis_index("seq")
    first_end = clip_ref[0, 0]
    second_end = first_end + clip_ref[0, 1]
    ends = (first_end, second_end, second_end + clip_ref[0, 2])
    for block in range(TOK // 128):
        start = seq * TOK + block * 128
        shape = (2 * 128, 2 * 128)
        k_axis = 0 if keys_first else 1
        k_at = lax.broadcasted_iota(jnp.int32, shape, k_axis)
        q_at = lax.rem(lax.broadcasted_iota(jnp.int32, shape, 1 - k_axis), 128)
        q_shape = (1, 256) if keys_first else (256, 1)
        k_shape = (256, 1) if keys_first else (1, 256)
        q_ids = clip_number(
            start + lax.rem(lax.broadcasted_iota(jnp.int32, q_shape, 1 - k_axis), 128),
            ends, group_len,
        )
        k_ids = clip_number(
            start - HALF + lax.broadcasted_iota(jnp.int32, k_shape, k_axis), ends, group_len
        )
        seen = (q_ids == k_ids) & (k_at >= q_at) & (k_at < q_at + 2 * HALF)
        bias_ref[block] = jnp.where(seen, 0.0, NEG)


def greet_sides(seq_count):
    dp, seq = lax.axis_index("dp"), lax.axis_index("seq")
    barrier = pltpu.get_barrier_semaphore()
    has_left, has_right = seq > 0, seq < seq_count - 1

    @pl.when(has_left)
    def _():
        pl.semaphore_signal(barrier, inc=1, device_id=(dp, seq - 1), device_id_type=MESH)

    @pl.when(has_right)
    def _():
        pl.semaphore_signal(barrier, inc=1, device_id=(dp, seq + 1), device_id_type=MESH)

    pl.semaphore_wait(barrier, has_left.astype(jnp.int32) + has_right.astype(jnp.int32))

    return (dp, seq - 1), (dp, seq + 1), has_left, has_right


def forward_kernel(
    seq_count, clip_ref, x_ref, gain_ref, gain_bias_ref, scale_ref, w_qkv, w_out, cos_all, sin_all,
    normed_ref, q_ref, kv_ref, att_ref, branch_ref,
    wq_v, wo_v, cos_v, sin_v, bias_v, load_sem, send_sem, recv_sem,
):
    dp, seq = lax.axis_index("dp"), lax.axis_index("seq")
    rows = pl.ds(pl.multiple_of(seq * TOK, TOK), TOK)
    copies = []
    order = [2, 3, 4, 5, 0, 1]
    tables = [
        pltpu.make_async_copy(cos_all.at[rows], cos_v, load_sem.at[0]),
        pltpu.make_async_copy(sin_all.at[rows], sin_v, load_sem.at[1]),
    ]
    chunks = {
        k: pltpu.make_async_copy(
            w_qkv.at[:, pl.ds(k * 512, 512)], wq_v.at[k], load_sem.at[2 + k]
        )
        for k in order
    }
    out_copy = pltpu.make_async_copy(w_out, wo_v, load_sem.at[8])
    for copy in tables + [chunks[k] for k in order] + [out_copy]:
        copy.start()
    left, right, has_left, has_right = greet_sides(seq_count)

    hat, _ = normalize(x_ref[...].astype(jnp.float32))
    normed_ref[...] = (hat * gain_ref[...] + gain_bias_ref[...]).astype(jnp.bfloat16)
    for copy in tables:
        copy.wait()

    def project(k):
        chunks[k].wait()
        for part in range(2):
            cols = slice(part * 256, part * 256 + 256)
            full = dot(normed_ref[...], wq_v[k, :, cols])
            for half in range(2):
                block = full[:, half * 128 : half * 128 + 128]
                at = (k % 2) * 512 + part * 256 + half * 128
                if k < 4:
                    block = rotated(block, cos_v[...], sin_v[...])
                block = block.astype(jnp.bfloat16)
                if k < 2:
                    q_ref[:, at : at + 128] = block
                else:
                    kv_ref[k // 2 - 1, HALF : HALF + TOK, at : at + 128] = block

    for k in order[:4]:
        project(k)

    to_left = pltpu.make_async_remote_copy(
        src_ref=kv_ref.at[:, pl.ds(HALF, HALF)], dst_ref=kv_ref.at[:, pl.ds(HALF + TOK, HALF)],
        send_sem=send_sem.at[0], recv_sem=recv_sem.at[0], device_id=left, device_id_type=MESH,
    )
    to_right = pltpu.make_async_remote_copy(
        src_ref=kv_ref.at[:, pl.ds(TOK, HALF)], dst_ref=kv_ref.at[:, pl.ds(0, HALF)],
        send_sem=send_sem.at[1], recv_sem=recv_sem.at[1], device_id=right, device_id_type=MESH,
    )

    @pl.when(has_left)
    def _():
        to_left.start()

    @pl.when(has_right)
    def _():
        to_right.start()

    @pl.when(jnp.logical_not(has_left))
    def _():
        kv_ref[:, 0:HALF] = jnp.zeros((2, HALF, D), jnp.bfloat16)

    @pl.when(jnp.logical_not(has_right))
    def _():
        kv_ref[:, HALF + TOK :] = jnp.zeros((2, HALF, D), jnp.bfloat16)

    for k in order[4:]:
        project(k)
    window_bias(bias_v, clip_ref, seq_count * TOK, False)

    heads = 4
    lanes_of = heads * HEAD_DIM

    def attend(blocks):
        def step(group, carry):
            lanes = pl.ds(pl.multiple_of(group * lanes_of, lanes_of), lanes_of)
            scores = []
            for block in blocks:
                queries = q_ref[block * 128 : block * 128 + 128, lanes] * 0.125
                keys = kv_ref[0, block * 128 : block * 128 + 256, lanes]
                bias = jnp.concatenate([bias_v[block]] * (heads // 2), 0)
                scores.append(contract_back(stacked_heads(queries, heads), keys) + bias)
            probs = []
            for score in scores:
                exponent = jnp.exp(score - jnp.max(score, -1, keepdims=True))
                total = jnp.sum(exponent, -1, keepdims=True)
                probs.append((exponent * (1.0 / total)).astype(jnp.bfloat16))
            for block, prob in zip(blocks, probs):
                values = kv_ref[1, block * 128 : block * 128 + 256, lanes]
                att_ref[block * 128 : block * 128 + 128, lanes] = merged_heads(
                    dot(prob, values), heads
                ).astype(jnp.bfloat16)
            return carry

        lax.fori_loop(0, D // lanes_of, step, 0)

    last = TOK // 128 - 1
    attend(list(range(1, last)))

    @pl.when(has_left)
    def _():
        to_right.wait_recv()

    @pl.when(has_right)
    def _():
        to_left.wait_recv()

    attend([0, last])
    out_copy.wait()
    for part in range(4):
        cols = slice(part * 256, part * 256 + 256)
        branch_ref[:, cols] = dot(att_ref[...], wo_v[:, cols])

    @pl.when(has_left)
    def _():
        to_left.wait_send()

    @pl.when(has_right)
    def _():
        to_right.wait_send()


def rotary_tables(group_len):
    half = HEAD_DIM // 2
    inv_freq = (10000.0 ** (-np.arange(half) / half)).astype(np.float32)[None, :]
    angles = np.arange(group_len, dtype=np.float32)[:, None] * inv_freq
    cosine, sine = np.cos(angles), np.sin(angles)
    return (
        np.concatenate([cosine] * 4, 1).astype(np.float32),
        np.concatenate([-sine, sine] * 2, 1).astype(np.float32),
    )


def forward_attention(frames, lengths, gain, bias, scale, w_qkv, w_out, tables, seq_count):
    bf, f32 = jnp.bfloat16, jnp.float32
    hbm = pl.BlockSpec(memory_space=pl.ANY)
    vmem = pl.BlockSpec(memory_space=pltpu.VMEM)
    smem = pl.BlockSpec(memory_space=pltpu.SMEM)
    shape = jax.ShapeDtypeStruct
    return pl.pallas_call(
        functools.partial(forward_kernel, seq_count),
        out_shape=[
            shape((TOK, D), bf),
            shape((TOK, D), bf),
            shape((2, TOK + 2 * HALF, D), bf),
            shape((TOK, D), bf),
            shape((TOK, D), f32),
        ],
        in_specs=[smem] + [vmem] * 4 + [hbm] * 4,
        out_specs=[vmem] * 5,
        scratch_shapes=[
            pltpu.VMEM((6, D, 512), bf),
            pltpu.VMEM((D, D), bf),
            pltpu.VMEM((TOK, 128), f32),
            pltpu.VMEM((TOK, 128), f32),
            pltpu.VMEM((TOK // 128, 256, 256), f32),
            pltpu.SemaphoreType.DMA((9,)),
            pltpu.SemaphoreType.DMA((2,)),
            pltpu.SemaphoreType.DMA((2,)),
        ],
        compiler_params=pltpu.CompilerParams(
            collective_id=2, has_side_effects=True, vmem_limit_bytes=48 * 2**20
        ),
        name="attention_forward",
    )(lengths, frames, gain[None], bias[None], scale[None], w_qkv, w_out, *tables)


FBLK = 512


def mlp_kernel(
    x_ref, c_ref, branch_ref, gain_ref, bias_ref, scale_attn_ref, scale_mlp_ref, w_gate_up, w_down,
    out_ref, n2_ref, hidden_ref, dgu_ref, dm_ref, db_ref, dmid_ref, vec_ref,
    wg_v, wu_v, wd_v, mlp_v, dn_v, load_sem,
):
    count = FF // FBLK

    def copies(step, slot):
        at = pl.multiple_of(step * FBLK, FBLK)
        return [
            pltpu.make_async_copy(
                w_gate_up.at[:, pl.ds(at, FBLK)], wg_v.at[slot], load_sem.at[slot, 0]
            ),
            pltpu.make_async_copy(
                w_gate_up.at[:, pl.ds(FF + at, FBLK)], wu_v.at[slot], load_sem.at[slot, 1]
            ),
            pltpu.make_async_copy(
                w_down.at[pl.ds(at, FBLK)], wd_v.at[slot], load_sem.at[slot, 2]
            ),
        ]

    for copy in copies(0, 0):
        copy.start()
    middle = x_ref[...].astype(jnp.float32) + scale_attn_ref[...] * branch_ref[...]
    hat, inverse = normalize(middle)
    n2_ref[...] = (hat * gain_ref[...] + bias_ref[...]).astype(jnp.bfloat16)
    dm_ref[...] = (c_ref[...].astype(jnp.float32) * scale_mlp_ref[...]).astype(jnp.bfloat16)
    mlp_v[...] = jnp.zeros_like(mlp_v)
    dn_v[...] = jnp.zeros_like(dn_v)

    def step(number, carry):
        slot = lax.rem(number, 2)

        @pl.when(number + 1 < count)
        def _():
            for copy in copies(number + 1, 1 - slot):
                copy.start()

        for copy in copies(number, slot):
            copy.wait()
        for part in range(FBLK // 256):
            cols = slice(part * 256, part * 256 + 256)
            at = pl.multiple_of(number * FBLK + part * 256, 256)
            gate = dot(n2_ref[...], wg_v[slot, :, cols])
            up = dot(n2_ref[...], wu_v[slot, :, cols])
            dh = contract_back(dm_ref[...], wd_v[slot, cols, :])
            sigmoid = 1.0 / (1.0 + jnp.exp(-gate))
            silu = gate * sigmoid
            hidden_ref[:, pl.ds(at, 256)] = (silu * up).astype(jnp.bfloat16)
            dgate = dh * up * (sigmoid * (1.0 + gate * (1.0 - sigmoid)))
            dgu_ref[:, pl.ds(at, 256)] = dgate.astype(jnp.bfloat16)
            dgu_ref[:, pl.ds(FF + at, 256)] = (dh * silu).astype(jnp.bfloat16)
        at = pl.multiple_of(number * FBLK, FBLK)
        mlp_v[...] += dot(hidden_ref[:, pl.ds(at, FBLK)], wd_v[slot])
        dn_v[...] += contract_back(dgu_ref[:, pl.ds(at, FBLK)], wg_v[slot]) + contract_back(
            dgu_ref[:, pl.ds(FF + at, FBLK)], wu_v[slot]
        )
        return carry

    lax.fori_loop(0, count, step, 0)
    cot = c_ref[...].astype(jnp.float32)
    branch = branch_ref[...]
    middle = x_ref[...].astype(jnp.float32) + scale_attn_ref[...] * branch
    mlp_out = mlp_v[...]
    out_ref[...] = (middle + scale_mlp_ref[...] * mlp_out).astype(jnp.bfloat16)
    vec_ref[0:1] = jnp.sum(cot * mlp_out, 0, keepdims=True)
    hat, inverse = normalize(middle)
    dn = dn_v[...]
    vec_ref[1:2] = jnp.sum(dn * hat, 0, keepdims=True)
    vec_ref[2:3] = jnp.sum(dn, 0, keepdims=True)
    dmid = cot + norm_backward(dn, hat, inverse, gain_ref[...])
    dmid_ref[...] = dmid
    vec_ref[3:4] = jnp.sum(dmid * branch, 0, keepdims=True)
    vec_ref[4:8] = jnp.zeros((4, D), jnp.float32)
    db_ref[...] = (dmid * scale_attn_ref[...]).astype(jnp.bfloat16)


def feed_forward(frames, cotangent, branch, gain, bias, scale_attn, scale_mlp, w_gate_up, w_down):
    bf, f32 = jnp.bfloat16, jnp.float32
    hbm = pl.BlockSpec(memory_space=pl.ANY)
    vmem = pl.BlockSpec(memory_space=pltpu.VMEM)
    shape = jax.ShapeDtypeStruct
    return pl.pallas_call(
        mlp_kernel,
        out_shape=[
            shape((TOK, D), bf),
            shape((TOK, D), bf),
            shape((TOK, FF), bf),
            shape((TOK, 2 * FF), bf),
            shape((TOK, D), bf),
            shape((TOK, D), bf),
            shape((TOK, D), f32),
            shape((8, D), f32),
        ],
        in_specs=[vmem] * 7 + [hbm] * 2,
        out_specs=[vmem] * 8,
        scratch_shapes=[
            pltpu.VMEM((2, D, FBLK), bf),
            pltpu.VMEM((2, D, FBLK), bf),
            pltpu.VMEM((2, FBLK, D), bf),
            pltpu.VMEM((TOK, D), f32),
            pltpu.VMEM((TOK, D), f32),
            pltpu.SemaphoreType.DMA((2, 3)),
        ],
        compiler_params=pltpu.CompilerParams(vmem_limit_bytes=56 * 2**20),
        name="feed_forward",
    )(
        frames, cotangent, branch, gain[None], bias[None], scale_attn[None], scale_mlp[None],
        w_gate_up, w_down,
    )


def backward_kernel(
    seq_count, clip_ref, x_ref, gain_ref, q_ref, kv_ref, db_ref, dmid_ref, w_qkv, w_out,
    cos_all, sin_all,
    dproj_ref, grad_ref, vec_ref,
    wq_v, wo_v, cos_v, sin_v, bias_v, datt_v, dkv_v, edge_v, far_v, load_sem, send_sem, recv_sem,
):
    seq = lax.axis_index("seq")
    rows = pl.ds(pl.multiple_of(seq * TOK, TOK), TOK)
    out_copy = pltpu.make_async_copy(w_out, wo_v, load_sem.at[8])
    tables = [
        pltpu.make_async_copy(cos_all.at[rows], cos_v, load_sem.at[0]),
        pltpu.make_async_copy(sin_all.at[rows], sin_v, load_sem.at[1]),
    ]
    chunks = [
        pltpu.make_async_copy(
            w_qkv.at[:, pl.ds(k * 512, 512)], wq_v.at[k], load_sem.at[2 + k]
        )
        for k in range(6)
    ]
    for copy in [out_copy] + tables + chunks:
        copy.start()
    left, right, has_left, has_right = greet_sides(seq_count)
    window_bias(bias_v, clip_ref, seq_count * TOK, True)
    out_copy.wait()
    for part in range(4):
        cols = slice(part * 256, part * 256 + 256)
        datt_v[:, cols] = contract_back(db_ref[...], wo_v[cols, :]).astype(jnp.bfloat16)
    for copy in tables:
        copy.wait()
    last = TOK // 128 - 1

    def attend(blocks):
        def step(pair, carry):
            lanes = pl.ds(pl.multiple_of(pair * 128, 128), 128)
            for block in blocks:
                own = slice(block * 128, block * 128 + 128)
                window = slice(block * 128, block * 128 + 256)
                queries = stacked(q_ref[own, lanes] * 0.125)
                grads = stacked(datt_v[own, lanes])
                keys = kv_ref[0, window, lanes]
                scores = contract_back(keys, queries) + bias_v[block]
                exponent = jnp.exp(scores - jnp.max(scores, 0, keepdims=True))
                total = jnp.sum(exponent, 0, keepdims=True)
                probs = exponent * (1.0 / total)
                d_probs = contract_back(kv_ref[1, window, lanes], grads)
                inner = jnp.sum(probs * d_probs, 0, keepdims=True)
                d_scores = (probs * (d_probs - inner)).astype(jnp.bfloat16)
                d_keys = dot(d_scores, queries)
                d_values = dot(probs.astype(jnp.bfloat16), grads)
                for which, update in ((0, d_keys), (1, d_values)):
                    if block in (0, last):
                        dkv_v[which, window, lanes] = update
                    elif block == 1:
                        dkv_v[which, 128:256, lanes] += update[:128]
                        dkv_v[which, 256:384, lanes] = update[128:]
                    else:
                        dkv_v[which, window, lanes] += update
                d_queries = merged(tn_dot(d_scores, keys)) * 0.125
                dproj_ref[own, lanes] = rotated(
                    d_queries, cos_v[own, :], -sin_v[own, :]
                ).astype(jnp.bfloat16)
            return carry

        lax.fori_loop(0, D // 128, step, 0)

    attend([0, last])
    edge_v[0] = dkv_v[:, 0:HALF].astype(jnp.bfloat16)
    edge_v[1] = dkv_v[:, HALF + TOK :].astype(jnp.bfloat16)
    to_left = pltpu.make_async_remote_copy(
        src_ref=edge_v.at[0], dst_ref=far_v.at[1],
        send_sem=send_sem.at[0], recv_sem=recv_sem.at[0], device_id=left, device_id_type=MESH,
    )
    to_right = pltpu.make_async_remote_copy(
        src_ref=edge_v.at[1], dst_ref=far_v.at[0],
        send_sem=send_sem.at[1], recv_sem=recv_sem.at[1], device_id=right, device_id_type=MESH,
    )

    @pl.when(has_left)
    def _():
        to_left.start()

    @pl.when(has_right)
    def _():
        to_right.start()

    attend(list(range(1, last)))

    @pl.when(has_left)
    def _():
        to_right.wait_recv()
        dkv_v[:, HALF : 2 * HALF] += far_v[0].astype(jnp.float32)

    @pl.when(has_right)
    def _():
        to_left.wait_recv()
        dkv_v[:, TOK : TOK + HALF] += far_v[1].astype(jnp.float32)

    for k in range(D // 128):
        lanes = slice(k * 128, k * 128 + 128)
        dproj_ref[:, D + k * 128 : D + k * 128 + 128] = rotated(
            dkv_v[0, HALF : HALF + TOK, lanes], cos_v[...], -sin_v[...]
        ).astype(jnp.bfloat16)
        dproj_ref[:, 2 * D + k * 128 : 2 * D + k * 128 + 128] = dkv_v[
            1, HALF : HALF + TOK, lanes
        ].astype(jnp.bfloat16)
    for copy in chunks:
        copy.wait()
    dn = contract_back(dproj_ref[:, 0:512], wq_v[0])
    for k in range(1, 6):
        dn += contract_back(dproj_ref[:, k * 512 : k * 512 + 512], wq_v[k])
    hat, inverse = normalize(x_ref[...].astype(jnp.float32))
    vec_ref[0:1] = jnp.sum(dn * hat, 0, keepdims=True)
    vec_ref[1:2] = jnp.sum(dn, 0, keepdims=True)
    vec_ref[2:8] = jnp.zeros((6, D), jnp.float32)
    grad_ref[...] = dmid_ref[...] + norm_backward(dn, hat, inverse, gain_ref[...])

    @pl.when(has_left)
    def _():
        to_left.wait_send()

    @pl.when(has_right)
    def _():
        to_right.wait_send()


def backward_attention(
    frames, lengths, gain, queries, kv, db, dmid, w_qkv, w_out, tables, seq_count
):
    bf, f32 = jnp.bfloat16, jnp.float32
    hbm = pl.BlockSpec(memory_space=pl.ANY)
    vmem = pl.BlockSpec(memory_space=pltpu.VMEM)
    smem = pl.BlockSpec(memory_space=pltpu.SMEM)
    shape = jax.ShapeDtypeStruct
    ext = TOK + 2 * HALF
    return pl.pallas_call(
        functools.partial(backward_kernel, seq_count),
        out_shape=[shape((TOK, 3 * D), bf), shape((TOK, D), f32), shape((8, D), f32)],
        in_specs=[smem] + [vmem] * 6 + [hbm] * 4,
        out_specs=[vmem] * 3,
        scratch_shapes=[
            pltpu.VMEM((6, D, 512), bf),
            pltpu.VMEM((D, D), bf),
            pltpu.VMEM((TOK, 128), f32),
            pltpu.VMEM((TOK, 128), f32),
            pltpu.VMEM((TOK // 128, 256, 256), f32),
            pltpu.VMEM((TOK, D), bf),
            pltpu.VMEM((2, ext, D), f32),
            pltpu.VMEM((2, 2, HALF, D), bf),
            pltpu.VMEM((2, 2, HALF, D), bf),
            pltpu.SemaphoreType.DMA((9,)),
            pltpu.SemaphoreType.DMA((2,)),
            pltpu.SemaphoreType.DMA((2,)),
        ],
        compiler_params=pltpu.CompilerParams(
            collective_id=3, has_side_effects=True, vmem_limit_bytes=56 * 2**20
        ),
        name="attention_backward",
    )(lengths, frames, gain[None], queries, kv, db, dmid, w_qkv, w_out, *tables)


RING = 8
COUNT = len(UNITS)


def stacked_heads(block, heads):
    lane = lax.broadcasted_iota(jnp.int32, block.shape, 1) // HEAD_DIM
    zero = jnp.zeros_like(block)
    return jnp.concatenate([jnp.where(lane == h, block, zero) for h in range(heads)], 0)


def merged_heads(rows, heads):
    lane = lax.broadcasted_iota(jnp.int32, (128, rows.shape[1]), 1) // HEAD_DIM
    total = rows[:128]
    for h in range(1, heads):
        total = jnp.where(lane == h, rows[128 * h : 128 * h + 128], total)
    return total


def layer_kernel(
    clip_ref, x_hbm, c_hbm, branch_hbm, q_hbm, kv_hbm, att_hbm, normed_hbm,
    gain1_ref, gain2_ref, bias2_ref, scale_attn_ref, scale_mlp_ref,
    w_qkv, w_out, w_gate_up, w_down, cos_all, sin_all,
    out_hbm, grad_hbm, out0, out1, out2, out3, vec_out, far_att, far_normed, hid_hbm, far_hid,
    part_a, part_b, part_c,
    recv_a1, recv_a2, recv_az, recv_b1, recv_b2, recv_bz, recv_cz, recv_c1, recv_c2,
    wide_v, deep_v, dkv_v, xbuf, ybuf, yfar, ydown, yout, other_v, hid_v,
    dm_v, db_v, datt_v, x_v, c_v, grad_v, q_v, kv_v, dproj_v, bias_v, cos_v, sin_v, edge_v, far_v,
    vec_sum, vec_recv, vec_z,
    send_sem, recv_sem, load_sem, far_send, far_recv, w_sem, hid_sem, hid_send, hid_recv,
    oth_send, oth_recv, q_send, q_recv, x_sem, edge_send, edge_recv, vec_send, vec_rsem, out_sem,
):
    outs = (out0, out1, out2, out3)
    dp = lax.axis_index("dp")
    seq = lax.axis_index("seq")
    z, y = dp // 2, dp % 2
    x, c = seq // 2, seq % 2
    dev_c = (dp, x * 2 + 1 - c)
    dev_x = (dp, (1 - x) * 2 + c)
    dev_y = (z * 2 + 1 - y, seq)
    dev_d = (dp, (1 - x) * 2 + 1 - c)
    dev_z = [(lax.rem(z + k, 4) * 2 + y, seq) for k in (1, 2, 3)]
    bf, f32 = jnp.bfloat16, jnp.float32

    def local_copy(src, dst, sem):
        return pltpu.make_async_copy(src, dst, sem)

    def remote(src, dst, ssem, rsem, device):
        return pltpu.make_async_remote_copy(
            src_ref=src, dst_ref=dst, send_sem=ssem, recv_sem=rsem,
            device_id=device, device_id_type=MESH,
        )

    def weights(step, slot):
        result = []
        for i in range(2):
            at = pl.multiple_of((c if i == 0 else 1 - c) * (FF // 2) + step * 256, 256)
            result += [
                local_copy(
                    w_gate_up.at[:, pl.ds(at, 256)], wide_v.at[4 * slot + i], w_sem.at[slot, i]
                ),
                local_copy(
                    w_gate_up.at[:, pl.ds(FF + at, 256)], wide_v.at[4 * slot + 2 + i],
                    w_sem.at[slot, 2 + i],
                ),
                local_copy(
                    w_down.at[pl.ds(at, 256)], deep_v.at[slot, pl.ds(256 * i, 256)],
                    w_sem.at[slot, 4 + i],
                ),
            ]
        return result

    rows = pl.ds(pl.multiple_of(seq * TOK, TOK), TOK)
    first = [
        local_copy(x_hbm, x_v, load_sem.at[0]),
        local_copy(branch_hbm, grad_v, load_sem.at[1]),
        local_copy(c_hbm, c_v, load_sem.at[2]),
    ]
    later = [
        local_copy(q_hbm, q_v, load_sem.at[3]),
        local_copy(kv_hbm, kv_v, load_sem.at[4]),
        local_copy(cos_all.at[rows], cos_v, load_sem.at[5]),
        local_copy(sin_all.at[rows], sin_v, load_sem.at[6]),
    ]
    for copy in first + weights(0, 0) + weights(1, 1):
        copy.start()

    barrier = pltpu.get_barrier_semaphore()
    for device in [dev_c, dev_x, dev_y, dev_d] + dev_z:
        pl.semaphore_signal(barrier, inc=1, device_id=device, device_id_type=MESH)
    pl.semaphore_wait(barrier, 7)

    is_end = (z == 0) | (z == 3)
    is_mid = (z == 1) | (z == 2)
    end_low = jnp.where(z == 0, 1, 0)
    end_dir = jnp.where(z == 0, 0, 1)
    end_next = (jnp.where(z == 0, 1, 2) * 2 + y, seq)
    mid_dir = jnp.where(z == 1, 0, 1)
    mid_low = jnp.where(z == 1, 1, 0)
    mid_keep = jnp.where(z == 1, 2, 0)
    mid_next = ((3 - z) * 2 + y, seq)
    back_dir = 1 - mid_dir
    back_low = jnp.where(z == 2, 2, 0)
    back_keep = jnp.where(z == 2, 3, 0)
    back_next = (jnp.where(z == 2, 3, 0) * 2 + y, seq)

    def z_send(slot, which, pieces, recv, number):
        ssem, rsem = send_sem.at[slot, which], recv_sem.at[slot, which]
        if number == 0:
            low, size, way, device = end_low, 3, end_dir, end_next
        elif number == 1:
            low, size, way, device = mid_keep, 2, mid_dir, mid_next
        else:
            low, size, way, device = back_keep, 1, back_dir, back_next
        return remote(
            pieces.at[pl.ds(low, size)], recv.at[way, pl.ds(low - 1 + way, size)],
            ssem.at[2 + number // 2], rsem.at[2 + way], device,
        )

    def z_wait(slot, which, recv, way, low, size):
        view = recv.at[way, pl.ds(low - 1 + way, size)]
        local_copy(view, view, recv_sem.at[slot, which, 2 + way]).wait()

    def z_round0(slot, which, pieces, recv):
        @pl.when(is_end)
        def _():
            z_send(slot, which, pieces, recv, 0).start()

    def z_round1(slot, which, pieces, recv):
        @pl.when(is_mid)
        def _():
            z_wait(slot, which, recv, mid_dir, mid_low, 3)
            keep = pl.ds(mid_keep, 2)
            pieces[keep] = pieces[keep] + recv[mid_dir, pl.ds(mid_keep - 1 + mid_dir, 2)]
            z_send(slot, which, pieces, recv, 1).start()

    def z_round2(slot, which, pieces, recv):
        @pl.when(is_mid)
        def _():
            z_wait(slot, which, recv, back_dir, back_low, 2)
            keep = pl.ds(back_keep, 1)
            pieces[keep] = pieces[keep] + recv[back_dir, pl.ds(back_keep - 1 + back_dir, 1)]
            z_send(slot, which, pieces, recv, 2).start()

    def z_final(slot, which, pieces, recv, finish):
        @pl.when(is_end)
        def _():
            way = 1 - end_dir
            z_wait(slot, which, recv, way, z, 1)
            finish(pieces[z].astype(f32) + recv[way, z - 1 + way].astype(f32))

        @pl.when(is_mid)
        def _():
            finish(
                pieces[z].astype(f32) + recv[0, z - 1].astype(f32) + recv[1, z].astype(f32)
            )

    def hop(slot, which, index):
        a, b, cc = part_a.at[slot], part_b.at[slot], part_c.at[slot]
        source, target, device = {
            (0, 0): lambda: (a.at[1 - x], recv_a1.at[slot], dev_x),
            (0, 1): lambda: (a.at[x, 1 - y], recv_a2.at[slot], dev_y),
            (1, 0): lambda: (b.at[1 - y], recv_b1.at[slot], dev_y),
            (1, 1): lambda: (b.at[y, 1 - x], recv_b2.at[slot], dev_x),
            (2, 0): lambda: (cc.at[z, 1 - x], recv_c1.at[slot], dev_x),
            (2, 1): lambda: (cc.at[z, x, 1 - y], recv_c2.at[slot], dev_y),
        }[which, index]()
        return remote(
            source, target, send_sem.at[slot, which, index], recv_sem.at[slot, which, index], device
        )

    def put(unit, which, block):
        _, _, _, _, _, offset, out, row = UNITS[unit]
        outs[out][row + PARTS[which] : row + PARTS[which + 1], offset : offset + 256] = block

    def stage(unit, number):
        slot = unit % RING if isinstance(unit, int) else lax.rem(unit, RING)
        a, b, cc = part_a.at[slot], part_b.at[slot], part_c.at[slot]
        a_z, b_z = a.at[x, y], b.at[y, x]
        rz_a, rz_b, rz_c = recv_az.at[slot], recv_bz.at[slot], recv_cz.at[slot]
        if number == 0:
            hop(slot, 0, 0).start()
            hop(slot, 1, 0).start()
            z_round0(slot, 2, cc, rz_c)
        if number == 1:
            hop(slot, 0, 0).wait_recv()
            a[x] = a[x] + recv_a1[slot]
            hop(slot, 0, 1).start()
            hop(slot, 1, 0).wait_recv()
            b[y] = b[y] + recv_b1[slot]
            hop(slot, 1, 1).start()
            z_round1(slot, 2, cc, rz_c)
        if number == 2:
            hop(slot, 0, 1).wait_recv()
            a[x, y] = a[x, y] + recv_a2[slot]
            z_round0(slot, 0, a_z, rz_a)
            hop(slot, 1, 1).wait_recv()
            b[y, x] = b[y, x] + recv_b2[slot]
            z_round0(slot, 1, b_z, rz_b)
            z_round2(slot, 2, cc, rz_c)
        if number == 3:
            z_round1(slot, 0, a_z, rz_a)
            z_round1(slot, 1, b_z, rz_b)

            def keep(value):
                cc[z] = value.astype(bf)

            z_final(slot, 2, cc, rz_c, keep)
            hop(slot, 2, 0).start()
        if number == 4:
            z_round2(slot, 0, a_z, rz_a)
            z_round2(slot, 1, b_z, rz_b)
            hop(slot, 2, 0).wait_recv()
            cc[z, x] = cc[z, x] + recv_c1[slot]
            hop(slot, 2, 1).start()
        if number == 5:
            z_final(slot, 0, a_z, rz_a, functools.partial(put, unit, 0))
            z_final(slot, 1, b_z, rz_b, functools.partial(put, unit, 1))
            hop(slot, 2, 1).wait_recv()
            put(unit, 2, cc[z, x, y].astype(f32) + recv_c2[slot].astype(f32))

    def sums(step):
        for number in range(1, 6):
            unit = step - number + 1
            if isinstance(step, int):
                if 0 <= unit < COUNT:
                    stage(unit, number)
            elif number < 5:

                @pl.when(unit >= 0)
                def _():
                    stage(unit, number)

    def sent(unit):
        slot = unit % RING
        for which in range(3):
            for index in range(2):
                hop(slot, which, index).wait_send()
        for which, (pieces, recv) in enumerate(
            (
                (part_a.at[slot, x, y], recv_az.at[slot]),
                (part_b.at[slot, y, x], recv_bz.at[slot]),
                (part_c.at[slot], recv_cz.at[slot]),
            )
        ):

            @pl.when(is_end)
            def _():
                z_send(slot, which, pieces, recv, 0).wait_send()

            @pl.when(is_mid)
            def _():
                z_send(slot, which, pieces, recv, 1).wait_send()
                z_send(slot, which, pieces, recv, 2).wait_send()

    def multiply(slot, xslot, own, far):
        def step(i, carry):
            columns = pl.ds(pl.multiple_of(i * 512, 512), 512)
            for xi in range(2):
                total = (
                    tn_dot(xbuf[xslot, 0, :, columns], own(xi))
                    + tn_dot(xbuf[xslot, 1, :, columns], far(xi))
                ).astype(bf)
                for k in range(4):
                    zi, yi = 2 * i + k // 2, k % 2
                    block = total[k * 128 : k * 128 + 128]
                    part_a[slot, xi, yi, zi] = block[PARTS[0] : PARTS[1]]
                    part_b[slot, yi, xi, zi] = block[PARTS[1] : PARTS[2]]
                    part_c[slot, zi, xi, yi] = block[PARTS[2] : PARTS[3]]
            return carry

        lax.fori_loop(0, 2, step, 0)

    def far_copy(src, dst, index):
        return remote(src, dst, far_send.at[index], far_recv.at[index], dev_c)

    def pair_columns(array, width, offset, core, xi):
        return array.at[:, pl.ds(pl.multiple_of((2 * xi + core) * width + offset, 256), 256)]

    far_n2 = far_copy(xbuf.at[0, 0], xbuf.at[0, 1], 0)
    far_a = far_copy(att_hbm, far_att, 1)
    far_n = far_copy(normed_hbm, far_normed, 2)
    far_dm = [
        far_copy(pair_columns(dm_v, 256, 0, 1 - c, xi), ydown.at[xi], 3 + xi) for xi in range(2)
    ]
    far_db = [
        far_copy(pair_columns(db_v, 256, 0, 1 - c, xi), yout.at[xi], 5 + xi) for xi in range(2)
    ]
    far_dq = [
        remote(
            pair_columns(dproj_v, 768, 256 * v, 1 - c, xi), yfar.at[v, xi],
            q_send.at[v, xi], q_recv.at[v, xi], dev_c,
        )
        for v in range(3)
        for xi in range(2)
    ]

    def far_other(step):
        return remote(
            other_v.at[lax.rem(step, 2)], yfar.at[lax.rem(step, 4)],
            oth_send.at[lax.rem(step, 2)], oth_recv.at[lax.rem(step, 4)], dev_c,
        )

    def hidden_copies(step):
        slot = lax.rem(step, 2)
        result = []
        for i in range(2):
            at = pl.multiple_of((c if i == 0 else 1 - c) * (FF // 2) + step * 256, 256)
            block = hid_v.at[slot, :, pl.ds(256 * i, 256)]
            result.append(local_copy(block, hid_hbm.at[:, pl.ds(at, 256)], hid_sem.at[slot, i]))
            result.append(
                remote(
                    block, far_hid.at[:, pl.ds(at, 256)],
                    hid_send.at[slot, i], hid_recv.at[step, i], dev_c,
                )
            )
        return result

    for copy in first:
        copy.wait()
    dkv_v[...] = jnp.zeros_like(dkv_v)
    vec_sum[0] = jnp.zeros((8, D), f32)

    def before(i, carry):
        at = pl.ds(pl.multiple_of(i * 128, 128), 128)
        middle = x_v[at, :].astype(f32) + scale_attn_ref[...] * grad_v[at, :]
        hat, _ = normalize(middle)
        xbuf[0, 0, at, :] = (hat * gain2_ref[...] + bias2_ref[...]).astype(bf)
        dm_v[at, :] = (c_v[at, :].astype(f32) * scale_mlp_ref[...]).astype(bf)
        return carry

    lax.fori_loop(0, TOK // 128, before, 0)
    for copy in [far_n2] + far_dm:
        copy.start()
    for copy in later:
        copy.start()

    def mlp(step):
        slot = lax.rem(step, 2)

        @pl.when(step >= 2)
        def _():
            far_other(step - 2).wait_send()
            for copy in hidden_copies(step - 2)[0::2]:
                copy.wait()
            for copy in hidden_copies(step - 2)[1::2]:
                copy.wait_send()

        for copy in weights(step, slot):
            copy.wait()
        normed = xbuf.at[0, 0]
        for i in range(2):
            gate = dot(normed[...], wide_v[4 * slot + i])
            up = dot(normed[...], wide_v[4 * slot + 2 + i])
            dh = contract_back(dm_v[...], deep_v[slot, 256 * i : 256 * i + 256])
            sigmoid = 1.0 / (1.0 + jnp.exp(-gate))
            silu = gate * sigmoid
            hid_v[slot, :, 256 * i : 256 * i + 256] = (silu * up).astype(bf)
            target = ybuf if i == 0 else other_v
            dgate = dh * up * (sigmoid * (1.0 + gate * (1.0 - sigmoid)))
            target[slot, 0] = dgate.astype(bf)
            target[slot, 1] = (dh * silu).astype(bf)
        far_other(step).start()
        for copy in hidden_copies(step):
            copy.start()
        dkv_v[0, 0:TOK] += dot(hid_v[slot], deep_v[slot])
        dkv_v[1, 0:TOK] += (
            contract_back(ybuf[slot, 0], wide_v[4 * slot])
            + contract_back(other_v[slot, 0], wide_v[4 * slot + 1])
            + contract_back(ybuf[slot, 1], wide_v[4 * slot + 2])
            + contract_back(other_v[slot, 1], wide_v[4 * slot + 3])
        )

        @pl.when(step + 2 < 8)
        def _():
            for copy in weights(step + 2, slot):
                copy.start()

    def gate_unit(step):
        far_other(step).wait_recv()
        multiply(
            step, 0, lambda xi: ybuf[lax.rem(step, 2), xi], lambda xi: yfar[lax.rem(step, 4), xi]
        )
        stage(step, 0)

    def mlp_step(step, carry):
        mlp(step)

        @pl.when(step == 0)
        def _():
            far_a.start()
            far_n.start()

        @pl.when(step == 1)
        def _():
            far_n2.wait_recv()

        @pl.when(step >= 1)
        def _():
            gate_unit(step - 1)

        @pl.when(step >= BEHIND)
        def _():
            sums(step - BEHIND)

        return carry

    lax.fori_loop(0, 8, mlp_step, 0)

    wo_copies = [
        local_copy(w_out.at[pl.ds(512 * k, 512)], deep_v.at[k], w_sem.at[k, 4]) for k in range(2)
    ]
    wq_copies = [
        local_copy(w_qkv.at[:, pl.ds(256 * k, 256)], wide_v.at[k % 8], w_sem.at[k % 8 // 4, k % 4])
        for k in range(12)
    ]
    for copy in wo_copies + wq_copies[:8]:
        copy.start()
    for step in (6, 7):
        far_other(step).wait_send()
        for copy in hidden_copies(step)[0::2]:
            copy.wait()
        for copy in hidden_copies(step)[1::2]:
            copy.wait_send()
    for step in range(8):
        for copy in hidden_copies(step)[1::2]:
            copy.wait_recv()

    def load_left(unit):
        left, offset, width, _, _, _, _, _ = UNITS[unit]
        slot = {8: 1, 9: 0, 10: 1, 11: 0, 12: 1, 13: 0}[unit]
        arrays = {3: (hid_hbm, far_hid), 1: (att_hbm, far_att), 0: (normed_hbm, far_normed)}[left]
        result = []
        for side in range(2):
            if width == 128:
                result.append(
                    local_copy(arrays[side], xbuf.at[slot, side], x_sem.at[slot, side, 0])
                )
                continue
            for block in range(8):
                result.append(
                    local_copy(
                        arrays[side].at[:, pl.ds(block * width + offset, 128)],
                        xbuf.at[slot, side, :, pl.ds(block * 128, 128)],
                        x_sem.at[slot, side, block],
                    )
                )
        return result

    def unit_sum(unit):
        if unit <= 13:
            for copy in load_left(unit):
                copy.wait()
        _, _, _, right, width, offset, _, _ = UNITS[unit]
        sent(unit - RING)
        slot, xslot = unit % RING, {8: 1, 9: 0, 10: 1, 11: 0, 12: 1}.get(unit, 0)
        own = {3: dm_v, 1: db_v, 0: dproj_v}[right]
        far = {3: ydown, 1: yout}.get(right, yfar.at[max(unit - 13, 0)])
        multiply(
            slot, xslot,
            lambda xi: pair_columns(own, width, offset, c, xi)[...],
            lambda xi: far[xi],
        )
        stage(unit, 0)
        if unit + 2 <= 13:
            if unit + 2 == 12:
                far_a.wait_recv()
            if unit + 2 == 13:
                far_n.wait_recv()
            for copy in load_left(unit + 2):
                copy.start()

    for copy in load_left(8):
        copy.start()
    gate_unit(7)
    for copy in [far_n2] + far_dm:
        copy.wait_send()
    for copy in load_left(9):
        copy.start()
    for copy in far_dm:
        copy.wait_recv()

    def after(i, carry):
        at = pl.ds(pl.multiple_of(i * 128, 128), 128)
        cot = c_v[at, :].astype(f32)
        branch = grad_v[at, :]
        middle = x_v[at, :].astype(f32) + scale_attn_ref[...] * branch
        mlp_out = dkv_v[0, at, :]
        dn = dkv_v[1, at, :]
        vec_sum[0, 5:6] += jnp.sum(cot * mlp_out, 0, keepdims=True)
        c_v[at, :] = (middle + scale_mlp_ref[...] * mlp_out).astype(bf)
        hat, inverse = normalize(middle)
        vec_sum[0, 3:4] += jnp.sum(dn * hat, 0, keepdims=True)
        vec_sum[0, 4:5] += jnp.sum(dn, 0, keepdims=True)
        dmid = cot + norm_backward(dn, hat, inverse, gain2_ref[...])
        vec_sum[0, 2:3] += jnp.sum(dmid * branch, 0, keepdims=True)
        grad_v[at, :] = dmid
        db_v[at, :] = (dmid * scale_attn_ref[...]).astype(bf)
        return carry

    out_copy = local_copy(c_v, out_hbm, out_sem.at[0])
    grad_copy = local_copy(grad_v, grad_hbm, out_sem.at[1])

    def norm_two_back():
        lax.fori_loop(0, TOK // 128, after, 0)
        out_copy.start()
        for copy in far_db:
            copy.start()

    def attended_grads():
        window_bias(bias_v, clip_ref, 4 * TOK, True)
        for k in range(2):
            wo_copies[k].wait()
        for k in range(2):
            datt_v[:, 512 * k : 512 * k + 512] = contract_back(db_v[...], deep_v[k]).astype(bf)
        for copy in far_db:
            copy.wait_recv()

    last = TOK // 128 - 1
    heads = 4
    lanes_of = heads * HEAD_DIM

    def attend(blocks):
        def step(group, carry):
            lanes = pl.ds(pl.multiple_of(group * lanes_of, lanes_of), lanes_of)
            held = []
            for block in blocks:
                own = slice(block * 128, block * 128 + 128)
                window = slice(block * 128, block * 128 + 256)
                queries = stacked_heads(q_v[own, lanes] * 0.125, heads)
                grads = stacked_heads(datt_v[own, lanes], heads)
                keys = kv_v[0, window, lanes]
                bias = jnp.concatenate([bias_v[block]] * (heads // 2), 1)
                scores = contract_back(keys, queries) + bias
                d_probs = contract_back(kv_v[1, window, lanes], grads)
                held.append((queries, grads, keys, scores, d_probs))
            ready = []
            for queries, grads, keys, scores, d_probs in held:
                exponent = jnp.exp(scores - jnp.max(scores, 0, keepdims=True))
                probs = exponent * (1.0 / jnp.sum(exponent, 0, keepdims=True))
                inner = jnp.sum(probs * d_probs, 0, keepdims=True)
                d_scores = (probs * (d_probs - inner)).astype(bf)
                ready.append((queries, grads, keys, d_scores, probs.astype(bf)))
            for block, (queries, grads, keys, d_scores, probs) in zip(blocks, ready):
                own = slice(block * 128, block * 128 + 128)
                window = slice(block * 128, block * 128 + 256)
                for which, update in ((0, dot(d_scores, queries)), (1, dot(probs, grads))):
                    if block in (0, last):
                        dkv_v[which, window, lanes] = update
                    elif block == 1:
                        dkv_v[which, 128:256, lanes] += update[:128]
                        dkv_v[which, 256:384, lanes] = update[128:]
                    else:
                        dkv_v[which, window, lanes] += update
                d_queries = merged_heads(tn_dot(d_scores, keys), heads) * 0.125
                for k in range(lanes_of // 128):
                    at = pl.ds(pl.multiple_of(group * lanes_of + 128 * k, 128), 128)
                    dproj_v[own, at] = rotated(
                        d_queries[:, 128 * k : 128 * k + 128], cos_v[own, :], -sin_v[own, :]
                    ).astype(bf)
            return carry

        lax.fori_loop(0, D // lanes_of, step, 0)

    has_left, has_right = seq > 0, seq < 3
    to_left = remote(
        edge_v.at[0], far_v.at[1], edge_send.at[0], edge_recv.at[0], (dp, seq - 1)
    )
    to_right = remote(
        edge_v.at[1], far_v.at[0], edge_send.at[1], edge_recv.at[1], (dp, seq + 1)
    )

    def edges_out():
        edge_v[0] = dkv_v[:, 0:HALF].astype(bf)
        edge_v[1] = dkv_v[:, HALF + TOK :].astype(bf)

        @pl.when(has_left)
        def _():
            to_left.start()

        @pl.when(has_right)
        def _():
            to_right.start()

    def edges_in():
        @pl.when(has_left)
        def _():
            to_right.wait_recv()
            dkv_v[:, HALF : 2 * HALF] += far_v[0].astype(f32)

        @pl.when(has_right)
        def _():
            to_left.wait_recv()
            dkv_v[:, TOK : TOK + HALF] += far_v[1].astype(f32)

        for k in range(D // 128):
            lanes = slice(k * 128, k * 128 + 128)
            dproj_v[:, D + k * 128 : D + k * 128 + 128] = rotated(
                dkv_v[0, HALF : HALF + TOK, lanes], cos_v[...], -sin_v[...]
            ).astype(bf)
            dproj_v[:, 2 * D + k * 128 : 2 * D + k * 128 + 128] = dkv_v[
                1, HALF : HALF + TOK, lanes
            ].astype(bf)
        for copy in far_dq:
            copy.start()

    def project_back(chunks, fresh):
        for k in chunks:
            wq_copies[k].wait()
        total = None
        for k in chunks:
            term = contract_back(dproj_v[:, 256 * k : 256 * k + 256], wide_v[k % 8])
            total = term if total is None else total + term
        if fresh:
            dkv_v[0, 0:TOK] = total
        else:
            dkv_v[0, 0:TOK] += total

    def last_norm(i, carry):
        at = pl.ds(pl.multiple_of(i * 128, 128), 128)
        hat, inverse = normalize(x_v[at, :].astype(f32))
        dn = dkv_v[0, at, :]
        vec_sum[0, 0:1] += jnp.sum(dn * hat, 0, keepdims=True)
        vec_sum[0, 1:2] += jnp.sum(dn, 0, keepdims=True)
        grad_v[at, :] += norm_backward(dn, hat, inverse, gain1_ref[...])
        return carry

    def norm_one_back():
        lax.fori_loop(0, TOK // 128, last_norm, 0)
        grad_copy.start()

    def vec_copy(number):
        return remote(
            vec_sum.at[number], vec_recv.at[number], vec_send.at[number], vec_rsem.at[number],
            (dev_c, dev_x, dev_y)[number],
        )

    vec_planes = [
        remote(vec_sum.at[3], vec_z.at[z], vec_send.at[3 + k], vec_rsem.at[3 + k], dev_z[k])
        for k in range(3)
    ]

    def vectors(number):
        if 0 < number <= 3:
            vec_copy(number - 1).wait_recv()
            vec_sum[number] = vec_sum[number - 1] + vec_recv[number - 1]
        if number < 3:
            vec_copy(number).start()
        elif number == 3:
            vec_z[z] = vec_sum[3]
            for copy in vec_planes:
                copy.start()
        else:
            for k in range(3):
                view = vec_z.at[lax.rem(z + 3 - k, 4)]
                local_copy(view, view, vec_rsem.at[3 + k]).wait()
            vec_out[...] = vec_z[0] + vec_z[1] + vec_z[2] + vec_z[3]

    def start_wq():
        for copy in wq_copies[8:]:
            copy.start()

    def far_dq_wait():
        for copy in far_dq:
            copy.wait_recv()

    actions = {
        "E": norm_two_back,
        "D": attended_grads,
        "A0": lambda: attend([0, last]),
        "O": edges_out,
        "A1": lambda: attend(list(range(1, last))),
        "I": edges_in,
        "W0": lambda: (project_back(range(8), True), start_wq()),
        "W1": lambda: project_back(range(8, 12), False),
        "N": norm_one_back,
        "Q": far_dq_wait,
    }
    for copy in later:
        copy.wait()
    for word in ORDER.split():
        if word in actions:
            actions[word]()
        elif word[0] == "P":
            unit_sum(int(word[1:]))
        elif word[0] == "S":
            sums(int(word[1:]))
        elif word[0] == "V":
            vectors(int(word[1:]))

    for unit in range(COUNT - RING, COUNT):
        sent(unit)
    for copy in [far_a, far_n] + far_db + far_dq + [vec_copy(k) for k in range(3)] + vec_planes:
        copy.wait_send()

    @pl.when(has_left)
    def _():
        to_left.wait_send()

    @pl.when(has_right)
    def _():
        to_right.wait_send()

    out_copy.wait()
    grad_copy.wait()


BEHIND = 4
ORDER = (
    "S4 P8 E S5 P9 D S6 P10 A0 O S7 P11 A1 I S8 P12 W0 S9 W1 Q P13 N S10 V0 P14 S11 V1 P15 S12 V2"
    " S13 V3 S14 V4 S15 S16 S17 S18 S19"
)


def layer(
    lengths, frames, cotangent, branch, queries, kv, attended, normed, vectors, w_qkv, w_out,
    w_gate_up, w_down, tables,
):
    bf, f32 = jnp.bfloat16, jnp.float32
    hbm = pl.BlockSpec(memory_space=pl.ANY)
    vmem = pl.BlockSpec(memory_space=pltpu.VMEM)
    smem = pl.BlockSpec(memory_space=pltpu.SMEM)
    shape = jax.ShapeDtypeStruct
    size = (PARTS[1], PARTS[2] - PARTS[1], PARTS[3] - PARTS[2])
    dma = pltpu.SemaphoreType.DMA
    ext = TOK + 2 * HALF
    scratch = [
        pltpu.VMEM((RING, 2, 2, 4, size[0], 256), bf),
        pltpu.VMEM((RING, 2, 2, 4, size[1], 256), bf),
        pltpu.VMEM((RING, 4, 2, 2, size[2], 256), bf),
        pltpu.VMEM((RING, 2, 4, size[0], 256), bf),
        pltpu.VMEM((RING, 4, size[0], 256), bf),
        pltpu.VMEM((RING, 2, 3, size[0], 256), bf),
        pltpu.VMEM((RING, 2, 4, size[1], 256), bf),
        pltpu.VMEM((RING, 4, size[1], 256), bf),
        pltpu.VMEM((RING, 2, 3, size[1], 256), bf),
        pltpu.VMEM((RING, 2, 3, 2, 2, size[2], 256), bf),
        pltpu.VMEM((RING, 2, size[2], 256), bf),
        pltpu.VMEM((RING, size[2], 256), bf),
        pltpu.VMEM((8, D, 256), bf),
        pltpu.VMEM((2, 512, D), bf),
        pltpu.VMEM((2, ext, D), f32),
        pltpu.VMEM((2, 2, TOK, D), bf),
        pltpu.VMEM((2, 2, TOK, 256), bf),
        pltpu.VMEM((4, 2, TOK, 256), bf),
        pltpu.VMEM((2, TOK, 256), bf),
        pltpu.VMEM((2, TOK, 256), bf),
        pltpu.VMEM((2, 2, TOK, 256), bf),
        pltpu.VMEM((2, TOK, 512), bf),
        pltpu.VMEM((TOK, D), bf),
        pltpu.VMEM((TOK, D), bf),
        pltpu.VMEM((TOK, D), bf),
        pltpu.VMEM((TOK, D), bf),
        pltpu.VMEM((TOK, D), bf),
        pltpu.VMEM((TOK, D), f32),
        pltpu.VMEM((TOK, D), bf),
        pltpu.VMEM((2, ext, D), bf),
        pltpu.VMEM((TOK, 3 * D), bf),
        pltpu.VMEM((TOK // 128, 256, 256), f32),
        pltpu.VMEM((TOK, 128), f32),
        pltpu.VMEM((TOK, 128), f32),
        pltpu.VMEM((2, 2, HALF, D), bf),
        pltpu.VMEM((2, 2, HALF, D), bf),
        pltpu.VMEM((4, 8, D), f32),
        pltpu.VMEM((3, 8, D), f32),
        pltpu.VMEM((4, 8, D), f32),
        dma((RING, 3, 4)),
        dma((RING, 3, 4)),
        dma((7,)),
        dma((7,)),
        dma((7,)),
        dma((2, 6)),
        dma((2, 2)),
        dma((2, 2)),
        dma((8, 2)),
        dma((2,)),
        dma((4,)),
        dma((3, 2)),
        dma((3, 2)),
        dma((2, 2, 8)),
        dma((2,)),
        dma((2,)),
        dma((6,)),
        dma((6,)),
        dma((2,)),
    ]
    return pl.pallas_call(
        layer_kernel,
        out_shape=[
            shape((TOK, D), bf),
            shape((TOK, D), f32),
            shape((128, 768), f32),
            shape((128, 256), f32),
            shape((128, 2048), f32),
            shape((512, 256), f32),
            shape((8, D), f32),
            shape((TOK, D), bf),
            shape((TOK, D), bf),
            shape((TOK, FF), bf),
            shape((TOK, FF), bf),
        ],
        in_specs=[smem] + [hbm] * 7 + [vmem] * 5 + [hbm] * 6,
        out_specs=[hbm] * 2 + [vmem] * 5 + [hbm] * 4,
        scratch_shapes=scratch,
        compiler_params=pltpu.CompilerParams(
            collective_id=4, has_side_effects=True, vmem_limit_bytes=64 * 2**20 - 2**16
        ),
        name="layer",
    )(
        lengths, frames, cotangent, branch, queries, kv, attended, normed,
        *[v[None] for v in vectors], w_qkv, w_out, w_gate_up, w_down, *tables,
    )[:7]


def local(
    frames,
    cotangent,
    clip_len,
    ln1_gain,
    ln1_bias,
    w_qkv,
    w_out,
    scale_attn,
    ln2_gain,
    ln2_bias,
    w_gate_up,
    w_down,
    scale_mlp,
):
    row_count = frames.shape[0]
    seq_count = lax.axis_size("seq")
    tables = rotary_tables(row_count * seq_count)
    normed_b, queries, kv, attended_t, branch = forward_attention(
        frames, clip_len, ln1_gain, ln1_bias, scale_attn, w_qkv, w_out, tables, seq_count
    )
    data_count = lax.axis_size("dp")
    if (data_count, seq_count, row_count) == (8, 4, TOK):
        out_frames, input_grad, sum_qkv, sum_out, sum_gate_up, sum_down, vector_total = layer(
            clip_len, frames, cotangent, branch, queries, kv, attended_t, normed_b,
            (ln1_gain, ln2_gain, ln2_bias, scale_attn, scale_mlp),
            w_qkv, w_out, w_gate_up, w_down, tables,
        )
    else:
        out_frames, normed_two_b, hidden_b, gate_up_b, mlp_grad, branch_grad, middle_grad, vec_two = (
            feed_forward(
                frames, cotangent, branch, ln2_gain, ln2_bias, scale_attn, scale_mlp, w_gate_up, w_down
            )
        )
        projected_grad, input_grad, vec_one = backward_attention(
            frames, clip_len, ln1_gain, queries, kv, branch_grad, middle_grad, w_qkv, w_out, tables,
            seq_count,
        )
        vector_grads = jnp.stack(
            [vec_one[0], vec_one[1], vec_two[3], vec_two[1], vec_two[2], vec_two[0]], 0
        )
        lefts = (normed_b, attended_t, normed_two_b, hidden_b)
        rights = (projected_grad, branch_grad, gate_up_b, mlp_grad)
        vector_total = lax.psum(vector_grads, ("dp", "seq"))
        sum_qkv, sum_out, sum_gate_up, sum_down = [
            lax.psum_scatter(
                to_blocks(contract_rows(left, right), data_count, seq_count),
                ("dp", "seq"),
                scatter_dimension=0,
                tiled=True,
            )[0]
            for left, right in zip(lefts, rights)
        ]
    return (
        out_frames,
        input_grad,
        vector_total[0],
        vector_total[1],
        sum_qkv,
        sum_out,
        vector_total[2],
        vector_total[3],
        vector_total[4],
        sum_gate_up,
        sum_down,
        vector_total[5],
    )


def solution(mesh):
    return jax.shard_map(
        local,
        mesh=mesh,
        in_specs=(
            P(("dp", "seq"), None),
            P(("dp", "seq"), None),
            P("dp", None),
            P(),
            P(),
            P(),
            P(),
            P(),
            P(),
            P(),
            P(),
            P(),
            P(),
        ),
        out_specs=(
            P(("dp", "seq"), None),
            P(("dp", "seq"), None),
            P(),
            P(),
            P("dp", "seq"),
            P("dp", "seq"),
            P(),
            P(),
            P(),
            P("dp", "seq"),
            P("dp", "seq"),
            P(),
        ),
        check_vma=False,
    )
```

profile of v0, /device:TPU:0, one launch (start us, length us, event | category | flops | bytes accessed | tf_op | source)
XLA Modules:
  0.0 197.1 jit_solution(5373536202205253776)
XLA Ops:
  0.6 0.0 copy-start
  0.7 1.2 copy-done
  1.9 0.0 copy-start.1
  1.9 1.2 copy-done.1
  3.1 0.0 copy-start.5
  3.1 0.7 copy-done.5
  3.8 0.0 copy-start.6
  3.8 0.7 copy-done.6
  4.5 0.0 copy-start.7
  4.5 0.7 copy-done.7
  5.2 0.0 copy-start.8
  5.2 0.7 copy-done.8
  5.8 17.9 %attention_forward.1 = (bf16[512,1024]{1,0:T(8,128)(2,1)S(1)}, bf16[512,1024]{1,0:T(8,128)(2,1)S(1)}, bf16[2,640,1024]{2,1,0:T(8,128)(2,1)}, bf16[512,1024]{1,0:T(8,128)(2,1)S(1)}, f32[512,1024]{1,0:T(8,128)}) custom-call(s32[1,3]{1,0:T(1,128)S(1)} %copy-done.8, bf16[512,1024]{1,0:T(8,128)(2,1)S(1)} %copy-done, f32[1,1024]{1,0:T(1,128)S(1)} %bitcast.13, ...), custom_call_target="tpu_custom_call" | custom-call | tf_op jit(solution)/shard_map/attention_forward/pallas_call | solution.py:301
  23.7 0.0 copy-start.2
  23.7 1.0 copy-done.2
  24.6 0.0 copy-start.3
  24.6 1.0 copy-done.3
  25.6 0.0 copy-start.4
  25.6 1.0 copy-done.4
  26.6 160.2 %layer.1 = (bf16[512,1024]{1,0:T(8,128)(2,1)}, f32[512,1024]{1,0:T(8,128)}, f32[128,768]{1,0:T(8,128)}, f32[128,256]{1,0:T(8,128)}, f32[128,2048]{1,0:T(8,128)},...) custom-call(s32[1,3]{1,0:T(1,128)} %clip_ref.3, ...), custom_call_target="tpu_custom_call" | custom-call | tf_op jit(solution)/shard_map/layer/pallas_call | solution.py:1389
  186.8 0.0 copy-start.11
  186.8 0.0 copy-start.12
  186.8 0.0 copy-start.9
  186.8 1.6 fusion
  188.4 2.3 %copy.33 = bf16[512,1024]{1,0:T(8,128)(2,1)} copy(bf16[512,1024]{1,0:T(8,128)(2,1)} %get-tuple-element.54) | data formatting | bytes 2097152
  190.7 0.0 copy-start.10
  190.7 3.2 %copy.34 = f32[512,1024]{1,0:T(8,128)} copy(f32[512,1024]{1,0:T(8,128)} %get-tuple-element.55) | data formatting | bytes 4194304
  193.9 0.0 copy-done.11
  193.9 0.7 copy.35
  194.6 0.0 copy-done.12
  194.6 0.7 copy.36
  195.3 0.0 copy-done.9
  195.3 1.0 copy.37
  196.3 0.0 copy-done.10
  196.3 0.8 copy.38
Async XLA Ops:
  0.6 1.2 copy-start
  1.9 1.2 copy-start.1
  3.1 0.7 copy-start.5
  3.8 0.7 copy-start.6
  4.5 0.7 copy-start.7
  5.2 0.7 copy-start.8
  23.7 1.0 copy-start.2
  24.6 1.0 copy-start.3
  25.6 1.0 copy-start.4
  186.8 7.1 %copy-start.11 = (f32[128,768]{1,0:T(8,128)S(1)}, f32[128,768]{1,0:T(8,128)}, u32[]{:S(2)}) copy-start(f32[128,768]{1,0:T(8,128)} %get-tuple-element.58) | copy-start | bytes 1179652
  186.8 7.9 %copy-start.12 = (f32[128,256]{1,0:T(8,128)S(1)}, f32[128,256]{1,0:T(8,128)}, u32[]{:S(2)}) copy-start(f32[128,256]{1,0:T(8,128)} %get-tuple-element.59) | copy-start | bytes 393220
  186.8 8.5 %copy-start.9 = (f32[128,2048]{1,0:T(8,128)S(1)}, f32[128,2048]{1,0:T(8,128)}, u32[]{:S(2)}) copy-start(f32[128,2048]{1,0:T(8,128)} %get-tuple-element.63) | copy-start | bytes 3145732
  190.7 5.6 %copy-start.10 = (f32[512,256]{1,0:T(8,128)S(1)}, f32[512,256]{1,0:T(8,128)}, u32[]{:S(2)}) copy-start(f32[512,256]{1,0:T(8,128)} %get-tuple-element.64) | copy-start | bytes 1572868
where the time goes:
time: 198 us; the launch traced here: 197 us
  Pallas kernels  178 us (90%)
  local copies, waits for them, and re-layouts  18.3 us (9%)
    pallas_call x1, Pallas kernels, layer(): pl.pallas_call(layer_kernel, out_shape=[shape((TOK, D), bf), shape((TOK,...  160 us
    pallas_call x1, Pallas kernels, forward_attention(): pl.pallas_call(functools.partial(forward_kernel, seq_count), out_shape=[s...  17.9 us
    unnamed x32, local copies, waits for them, and re-layouts  16.7 us

commit v1 on v0

--- a/solution.py
+++ b/solution.py
@@ -320,7 +320,7 @@
             pltpu.SemaphoreType.DMA((2,)),
         ],
         compiler_params=pltpu.CompilerParams(
-            collective_id=2, has_side_effects=True, vmem_limit_bytes=48 * 2**20
+            collective_id=2, has_side_effects=True, vmem_limit_bytes=56 * 2**20
         ),
         name="attention_forward",
     )(lengths, frames, gain[None], bias[None], scale[None], w_qkv, w_out, *tables)
@@ -620,17 +620,16 @@
 
 
 def layer_kernel(
-    clip_ref, x_hbm, c_hbm, branch_hbm, q_hbm, kv_hbm, att_hbm, normed_hbm,
-    gain1_ref, gain2_ref, bias2_ref, scale_attn_ref, scale_mlp_ref,
+    clip_ref, x_hbm, c_hbm, gain1_ref, bias1_ref, gain2_ref, bias2_ref, scale_attn_ref, scale_mlp_ref,
     w_qkv, w_out, w_gate_up, w_down, cos_all, sin_all,
-    out_hbm, grad_hbm, out0, out1, out2, out3, vec_out, far_att, far_normed, hid_hbm, far_hid,
+    out_hbm, grad_hbm, out0, out1, out2, out3, vec_out, att_hbm, normed_hbm, far_att, far_normed, hid_hbm, far_hid,
     part_a, part_b, part_c,
     recv_a1, recv_a2, recv_az, recv_b1, recv_b2, recv_bz, recv_cz, recv_c1, recv_c2,
     wide_v, deep_v, dkv_v, xbuf, ybuf, yfar, ydown, yout, other_v, hid_v,
     dm_v, db_v, datt_v, x_v, c_v, grad_v, q_v, kv_v, dproj_v, bias_v, cos_v, sin_v, edge_v, far_v,
     vec_sum, vec_recv, vec_z,
     send_sem, recv_sem, load_sem, far_send, far_recv, w_sem, hid_sem, hid_send, hid_recv,
-    oth_send, oth_recv, q_send, q_recv, x_sem, edge_send, edge_recv, vec_send, vec_rsem, out_sem,
+    oth_send, oth_recv, q_send, q_recv, x_sem, edge_send, edge_recv, vec_send, vec_rsem, out_sem, halo_send, halo_recv,
 ):
     outs = (out0, out1, out2, out3)
     dp = lax.axis_index("dp")
@@ -673,24 +672,42 @@
         return result
 
     rows = pl.ds(pl.multiple_of(seq * TOK, TOK), TOK)
-    first = [
-        local_copy(x_hbm, x_v, load_sem.at[0]),
-        local_copy(branch_hbm, grad_v, load_sem.at[1]),
-        local_copy(c_hbm, c_v, load_sem.at[2]),
+    x_copy = local_copy(x_hbm, x_v, load_sem.at[0])
+    c_copy = local_copy(c_hbm, c_v, load_sem.at[1])
+    tables = [
+        local_copy(cos_all.at[rows], cos_v, load_sem.at[2]),
+        local_copy(sin_all.at[rows], sin_v, load_sem.at[3]),
     ]
-    later = [
-        local_copy(q_hbm, q_v, load_sem.at[3]),
-        local_copy(kv_hbm, kv_v, load_sem.at[4]),
-        local_copy(cos_all.at[rows], cos_v, load_sem.at[5]),
-        local_copy(sin_all.at[rows], sin_v, load_sem.at[6]),
+    wo_first = [
+        local_copy(
+            w_out.at[pl.ds(512 * k, 512)], dproj_v.at[:, pl.ds(D * k, D)], load_sem.at[4 + k]
+        )
+        for k in range(2)
     ]
-    for copy in first + weights(0, 0) + weights(1, 1):
+    wq_copies = [
+        local_copy(w_qkv.at[:, pl.ds(256 * k, 256)], wide_v.at[k % 8], w_sem.at[k % 8 // 4, k % 4])
+        for k in range(12)
+    ]
+    wq_first = {
+        k: local_copy(
+            w_qkv.at[:, pl.ds(256 * k, 256)], wide_v.at[k - 4 if k >= 4 else k],
+            w_sem.at[k // 8, k % 4],
+        )
+        for k in [4, 5, 6, 7, 8, 9, 10, 11, 0, 1, 2, 3]
+    }
+    x_copy.start()
+    for k in range(4, 8):
+        wq_first[k].start()
+    for copy in tables:
+        copy.start()
+    for k in range(8, 12):
+        wq_first[k].start()
+    for copy in wo_first + [c_copy]:
         copy.start()
 
     barrier = pltpu.get_barrier_semaphore()
     for device in [dev_c, dev_x, dev_y, dev_d] + dev_z:
         pl.semaphore_signal(barrier, inc=1, device_id=device, device_id_type=MESH)
-    pl.semaphore_wait(barrier, 7)
 
     is_end = (z == 0) | (z == 3)
     is_mid = (z == 1) | (z == 2)
@@ -772,6 +789,10 @@
         )
 
     def put(unit, which, block):
+        if not isinstance(unit, int):
+            columns = pl.ds(pl.multiple_of(unit * 256, 256), 256)
+            out2[PARTS[which] : PARTS[which + 1], columns] = block
+            return
         _, _, _, _, _, offset, out, row = UNITS[unit]
         outs[out][row + PARTS[which] : row + PARTS[which + 1], offset : offset + 256] = block
 
@@ -827,7 +848,7 @@
             if isinstance(step, int):
                 if 0 <= unit < COUNT:
                     stage(unit, number)
-            elif number < 5:
+            else:
 
                 @pl.when(unit >= 0)
                 def _():
@@ -880,8 +901,8 @@
         return array.at[:, pl.ds(pl.multiple_of((2 * xi + core) * width + offset, 256), 256)]
 
     far_n2 = far_copy(xbuf.at[0, 0], xbuf.at[0, 1], 0)
-    far_a = far_copy(att_hbm, far_att, 1)
-    far_n = far_copy(normed_hbm, far_normed, 2)
+    far_a = far_copy(xbuf.at[1, 1], far_att, 1)
+    far_n = far_copy(xbuf.at[1, 0], far_normed, 2)
     far_dm = [
         far_copy(pair_columns(dm_v, 256, 0, 1 - c, xi), ydown.at[xi], 3 + xi) for xi in range(2)
     ]
@@ -918,24 +939,146 @@
             )
         return result
 
-    for copy in first:
+    window_bias(bias_v, clip_ref, 4 * TOK, True)
+    vec_sum[0] = jnp.zeros((8, D), f32)
+    x_copy.wait()
+
+    def first_norm(i, carry):
+        at = pl.ds(pl.multiple_of(i * 128, 128), 128)
+        hat, _ = normalize(x_v[at, :].astype(f32))
+        xbuf[1, 0, at, :] = (hat * gain1_ref[...] + bias1_ref[...]).astype(bf)
+        return carry
+
+    lax.fori_loop(0, TOK // 128, first_norm, 0)
+    normed_copy = local_copy(xbuf.at[1, 0], normed_hbm, out_sem.at[2])
+    att_copy = local_copy(xbuf.at[1, 1], att_hbm, out_sem.at[3])
+    normed_copy.start()
+    for copy in tables:
         copy.wait()
+
+    def project(k):
+        full = dot(xbuf[1, 0], wide_v[k - 4 if k >= 4 else k])
+        for half in range(2):
+            block = full[:, half * 128 : half * 128 + 128]
+            at = (k % 4) * 256 + half * 128
+            if k < 8:
+                block = rotated(block, cos_v[...], sin_v[...])
+            block = block.astype(bf)
+            if k < 4:
+                q_v[:, at : at + 128] = block
+            else:
+                kv_v[k // 4 - 1, HALF : HALF + TOK, at : at + 128] = block
+
+    def project_all(chunks):
+        for k in chunks:
+            wq_first[k].wait()
+        for k in chunks:
+            project(k)
+
+    project_all(range(4, 8))
+    for k in range(4):
+        wq_first[k].start()
+    project_all(range(8, 12))
+    pl.semaphore_wait(barrier, 7)
+    has_left, has_right = seq > 0, seq < 3
+    halo_left = remote(
+        kv_v.at[:, pl.ds(HALF, HALF)], kv_v.at[:, pl.ds(HALF + TOK, HALF)],
+        halo_send.at[0], halo_recv.at[0], (dp, seq - 1),
+    )
+    halo_right = remote(
+        kv_v.at[:, pl.ds(TOK, HALF)], kv_v.at[:, pl.ds(0, HALF)],
+        halo_send.at[1], halo_recv.at[1], (dp, seq + 1),
+    )
+
+    @pl.when(has_left)
+    def _():
+        halo_left.start()
+
+    @pl.when(has_right)
+    def _():
+        halo_right.start()
+
+    @pl.when(jnp.logical_not(has_left))
+    def _():
+        kv_v[:, 0:HALF] = jnp.zeros((2, HALF, D), bf)
+
+    @pl.when(jnp.logical_not(has_right))
+    def _():
+        kv_v[:, HALF + TOK :] = jnp.zeros((2, HALF, D), bf)
+
+    far_n.start()
+    project_all(range(4))
+    for copy in weights(0, 0) + weights(1, 1):
+        copy.start()
+    last = TOK // 128 - 1
+    heads = 4
+    lanes_of = heads * HEAD_DIM
+
+    def attend_forward(blocks):
+        def step(group, carry):
+            lanes = pl.ds(pl.multiple_of(group * lanes_of, lanes_of), lanes_of)
+            scores = []
+            for block in blocks:
+                queries = q_v[block * 128 : block * 128 + 128, lanes] * 0.125
+                keys = kv_v[0, block * 128 : block * 128 + 256, lanes]
+                bias = jnp.concatenate([bias_v[block]] * (heads // 2), 1)
+                scores.append(contract_back(keys, stacked_heads(queries, heads)) + bias)
+            probs = []
+            for score in scores:
+                exponent = jnp.exp(score - jnp.max(score, 0, keepdims=True))
+                total = jnp.sum(exponent, 0, keepdims=True)
+                probs.append((exponent * (1.0 / total)).astype(bf))
+            for block, prob in zip(blocks, probs):
+                values = kv_v[1, block * 128 : block * 128 + 256, lanes]
+                xbuf[1, 1, block * 128 : block * 128 + 128, lanes] = merged_heads(
+                    tn_dot(prob, values), heads
+                ).astype(bf)
+            return carry
+
+        lax.fori_loop(0, D // lanes_of, step, 0)
+
+    attend_forward(list(range(1, last)))
+    c_copy.wait()
+
+    def scaled(i, carry):
+        at = pl.ds(pl.multiple_of(i * 128, 128), 128)
+        dm_v[at, :] = (c_v[at, :].astype(f32) * scale_mlp_ref[...]).astype(bf)
+        return carry
+
+    lax.fori_loop(0, TOK // 128, scaled, 0)
+    for copy in far_dm:
+        copy.start()
     dkv_v[...] = jnp.zeros_like(dkv_v)
-    vec_sum[0] = jnp.zeros((8, D), f32)
+
+    @pl.when(has_left)
+    def _():
+        halo_right.wait_recv()
+
+    @pl.when(has_right)
+    def _():
+        halo_left.wait_recv()
+
+    attend_forward([0, last])
+    att_copy.start()
+    far_a.start()
+    for copy in wo_first:
+        copy.wait()
+    for part in range(4):
+        cols = slice(part * 256, part * 256 + 256)
+        grad_v[:, cols] = dot(xbuf[1, 1, :, 0:512], dproj_v[:, cols]) + dot(
+            xbuf[1, 1, :, 512:1024], dproj_v[:, D + part * 256 : D + part * 256 + 256]
+        )
+
 
     def before(i, carry):
         at = pl.ds(pl.multiple_of(i * 128, 128), 128)
         middle = x_v[at, :].astype(f32) + scale_attn_ref[...] * grad_v[at, :]
         hat, _ = normalize(middle)
         xbuf[0, 0, at, :] = (hat * gain2_ref[...] + bias2_ref[...]).astype(bf)
-        dm_v[at, :] = (c_v[at, :].astype(f32) * scale_mlp_ref[...]).astype(bf)
         return carry
 
     lax.fori_loop(0, TOK // 128, before, 0)
-    for copy in [far_n2] + far_dm:
-        copy.start()
-    for copy in later:
-        copy.start()
+    far_n2.start()
 
     def mlp(step):
         slot = lax.rem(step, 2)
@@ -990,16 +1133,9 @@
 
         @pl.when(step == 0)
         def _():
-            far_a.start()
-            far_n.start()
-
-        @pl.when(step == 1)
-        def _():
             far_n2.wait_recv()
 
-        @pl.when(step >= 1)
-        def _():
-            gate_unit(step - 1)
+        gate_unit(step)
 
         @pl.when(step >= BEHIND)
         def _():
@@ -1011,10 +1147,6 @@
 
     wo_copies = [
         local_copy(w_out.at[pl.ds(512 * k, 512)], deep_v.at[k], w_sem.at[k, 4]) for k in range(2)
-    ]
-    wq_copies = [
-        local_copy(w_qkv.at[:, pl.ds(256 * k, 256)], wide_v.at[k % 8], w_sem.at[k % 8 // 4, k % 4])
-        for k in range(12)
     ]
     for copy in wo_copies + wq_copies[:8]:
         copy.start()
@@ -1054,7 +1186,8 @@
             for copy in load_left(unit):
                 copy.wait()
         _, _, _, right, width, offset, _, _ = UNITS[unit]
-        sent(unit - RING)
+        if unit >= RING:
+            sent(unit - RING)
         slot, xslot = unit % RING, {8: 1, 9: 0, 10: 1, 11: 0, 12: 1}.get(unit, 0)
         own = {3: dm_v, 1: db_v, 0: dproj_v}[right]
         far = {3: ydown, 1: yout}.get(right, yfar.at[max(unit - 13, 0)])
@@ -1072,11 +1205,12 @@
             for copy in load_left(unit + 2):
                 copy.start()
 
+    for copy in [far_n2, far_a, far_n] + far_dm:
+        copy.wait_send()
+    normed_copy.wait()
+    att_copy.wait()
     for copy in load_left(8):
         copy.start()
-    gate_unit(7)
-    for copy in [far_n2] + far_dm:
-        copy.wait_send()
     for copy in load_left(9):
         copy.start()
     for copy in far_dm:
@@ -1110,17 +1244,12 @@
             copy.start()
 
     def attended_grads():
-        window_bias(bias_v, clip_ref, 4 * TOK, True)
         for k in range(2):
             wo_copies[k].wait()
         for k in range(2):
             datt_v[:, 512 * k : 512 * k + 512] = contract_back(db_v[...], deep_v[k]).astype(bf)
         for copy in far_db:
             copy.wait_recv()
-
-    last = TOK // 128 - 1
-    heads = 4
-    lanes_of = heads * HEAD_DIM
 
     def attend(blocks):
         def step(group, carry):
@@ -1164,7 +1293,6 @@
 
         lax.fori_loop(0, D // lanes_of, step, 0)
 
-    has_left, has_right = seq > 0, seq < 3
     to_left = remote(
         edge_v.at[0], far_v.at[1], edge_send.at[0], edge_recv.at[0], (dp, seq - 1)
     )
@@ -1278,8 +1406,6 @@
         "N": norm_one_back,
         "Q": far_dq_wait,
     }
-    for copy in later:
-        copy.wait()
     for word in ORDER.split():
         if word in actions:
             actions[word]()
@@ -1292,15 +1418,17 @@
 
     for unit in range(COUNT - RING, COUNT):
         sent(unit)
-    for copy in [far_a, far_n] + far_db + far_dq + [vec_copy(k) for k in range(3)] + vec_planes:
+    for copy in far_db + far_dq + [vec_copy(k) for k in range(3)] + vec_planes:
         copy.wait_send()
 
     @pl.when(has_left)
     def _():
+        halo_left.wait_send()
         to_left.wait_send()
 
     @pl.when(has_right)
     def _():
+        halo_right.wait_send()
         to_right.wait_send()
 
     out_copy.wait()
@@ -1315,8 +1443,7 @@
 
 
 def layer(
-    lengths, frames, cotangent, branch, queries, kv, attended, normed, vectors, w_qkv, w_out,
-    w_gate_up, w_down, tables,
+    lengths, frames, cotangent, vectors, w_qkv, w_out, w_gate_up, w_down, tables,
 ):
     bf, f32 = jnp.bfloat16, jnp.float32
     hbm = pl.BlockSpec(memory_space=pl.ANY)
@@ -1384,9 +1511,11 @@
         dma((2,)),
         dma((6,)),
         dma((6,)),
+        dma((4,)),
+        dma((2,)),
         dma((2,)),
     ]
-    return pl.pallas_call(
+    results = pl.pallas_call(
         layer_kernel,
         out_shape=[
             shape((TOK, D), bf),
@@ -1396,22 +1525,53 @@
             shape((128, 2048), f32),
             shape((512, 256), f32),
             shape((8, D), f32),
-            shape((TOK, D), bf),
-            shape((TOK, D), bf),
+        ]
+        + [shape((TOK, D), bf)] * 4
+        + [
             shape((TOK, FF), bf),
             shape((TOK, FF), bf),
         ],
-        in_specs=[smem] + [hbm] * 7 + [vmem] * 5 + [hbm] * 6,
-        out_specs=[hbm] * 2 + [vmem] * 5 + [hbm] * 4,
+        in_specs=[smem] + [hbm] * 2 + [vmem] * 6 + [hbm] * 6,
+        out_specs=[hbm] * 2 + [vmem] * 5 + [hbm] * 6,
         scratch_shapes=scratch,
         compiler_params=pltpu.CompilerParams(
             collective_id=4, has_side_effects=True, vmem_limit_bytes=64 * 2**20 - 2**16
         ),
         name="layer",
     )(
-        lengths, frames, cotangent, branch, queries, kv, attended, normed,
-        *[v[None] for v in vectors], w_qkv, w_out, w_gate_up, w_down, *tables,
+        lengths, frames, cotangent, *[v[None] for v in vectors], w_qkv, w_out, w_gate_up, w_down, *tables,
     )[:7]
+    finished = pl.pallas_call(
+        finish_kernel,
+        out_shape=[shape(v.shape, v.dtype) for v in results[:6]] + [shape((1, D), f32)] * 6,
+        in_specs=[hbm] * 6 + [vmem],
+        out_specs=[hbm] * 6 + [vmem] * 6,
+        scratch_shapes=[pltpu.VMEM(v.shape, v.dtype) for v in results[:6]] + [dma((2, 6))],
+        compiler_params=pltpu.CompilerParams(vmem_limit_bytes=64 * 2**20 - 2**16),
+        name="finish",
+    )(*results)
+    return finished[:6], [v[0] for v in finished[6:]]
+
+
+def finish_kernel(*refs):
+    sources, targets, held, sems = refs[:6], refs[7:13], refs[19:25], refs[25]
+    arrivals = [
+        pltpu.make_async_copy(source, target, sems.at[0, k])
+        for k, (source, target) in enumerate(zip(sources, held))
+    ]
+    departures = [
+        pltpu.make_async_copy(source, target, sems.at[1, k])
+        for k, (source, target) in enumerate(zip(held, targets))
+    ]
+    for copy in arrivals:
+        copy.start()
+    for k in range(6):
+        refs[13 + k][...] = refs[6][k : k + 1]
+    for arrival, departure in zip(arrivals, departures):
+        arrival.wait()
+        departure.start()
+    for copy in departures:
+        copy.wait()
 
 
 def local(
@@ -1432,17 +1592,18 @@
     row_count = frames.shape[0]
     seq_count = lax.axis_size("seq")
     tables = rotary_tables(row_count * seq_count)
-    normed_b, queries, kv, attended_t, branch = forward_attention(
-        frames, clip_len, ln1_gain, ln1_bias, scale_attn, w_qkv, w_out, tables, seq_count
-    )
     data_count = lax.axis_size("dp")
     if (data_count, seq_count, row_count) == (8, 4, TOK):
-        out_frames, input_grad, sum_qkv, sum_out, sum_gate_up, sum_down, vector_total = layer(
-            clip_len, frames, cotangent, branch, queries, kv, attended_t, normed_b,
-            (ln1_gain, ln2_gain, ln2_bias, scale_attn, scale_mlp),
+        sums, vector_total = layer(
+            clip_len, frames, cotangent,
+            (ln1_gain, ln1_bias, ln2_gain, ln2_bias, scale_attn, scale_mlp),
             w_qkv, w_out, w_gate_up, w_down, tables,
         )
+        out_frames, input_grad, sum_qkv, sum_out, sum_gate_up, sum_down = sums
     else:
+        normed_b, queries, kv, attended_t, branch = forward_attention(
+            frames, clip_len, ln1_gain, ln1_bias, scale_attn, w_qkv, w_out, tables, seq_count
+        )
         out_frames, normed_two_b, hidden_b, gate_up_b, mlp_grad, branch_grad, middle_grad, vec_two = (
             feed_forward(
                 frames, cotangent, branch, ln2_gain, ln2_bias, scale_attn, scale_mlp, w_gate_up, w_down

time: 198 us -> 180 us (0.909)
  local copies, waits for them, and re-layouts: 18.3 us -> 0 us
    unnamed x32 -> x0, local copies, waits for them, and re-layouts: 16.7 us -> none
    pallas_call x1, Pallas kernels: 160 us -> 174 us  [layer(): pl.pallas_call(layer_kernel, out_shape=[shape((TOK, D), bf), shape((TOK,...]
    pallas_call x1, Pallas kernels: 17.9 us -> 5.4 us  [layer(): pl.pallas_call(finish_kernel, out_shape=[shape(v.shape, v.dtype) for v in...]
where the time goes in v1:
time: 180 us
  Pallas kernels  179 us (99%)
    pallas_call x1, Pallas kernels, layer(): pl.pallas_call(layer_kernel, out_shape=[shape((TOK, D), bf), shape((TOK,...  174 us
    pallas_call x1, Pallas kernels, layer(): pl.pallas_call(finish_kernel, out_shape=[shape(v.shape, v.dtype) for v in...  5.4 us

profile of v1, /device:TPU:0, one launch (start us, length us, event | category | flops | bytes accessed | tf_op | source)
XLA Modules:
  0.0 180.2 jit_solution(16303784458231299130)
XLA Ops:
  0.6 174.0 %layer.1 = (bf16[512,1024]{1,0:T(8,128)(2,1)}, f32[512,1024]{1,0:T(8,128)}, f32[128,768]{1,0:T(8,128)}, f32[128,256]{1,0:T(8,128)}, f32[128,2048]{1,0:T(8,128)},...) custom-call(s32[1,3]{1,0:T(1,128)} %clip_ref.1, ...), custom_call_target="tpu_custom_call" | custom-call | tf_op jit(solution)/shard_map/layer/pallas_call | solution.py:1518
  174.6 5.4 %finish.1 = (bf16[512,1024]{1,0:T(8,128)(2,1)}, f32[512,1024]{1,0:T(8,128)}, f32[128,768]{1,0:T(8,128)}, f32[128,256]{1,0:T(8,128)}, f32[128,2048]{1,0:T(8,128)}...) custom-call(bf16[512,1024]{1,0:T(8,128)(2,1)} %get-tuple-element.31., ...), custom_call_target="tpu_custom_call" | custom-call | tf_op jit(solution)/shard_map/finish/pallas_call | solution.py:1544

commit v2 on v1

--- a/solution.py
+++ b/solution.py
@@ -43,6 +43,8 @@
 MESH = pl.DeviceIdType.MESH
 TOK = 512
 PARTS = (0, 48, 96, 128)
+LAST_PARTS = (0, 64, 128, 128)
+LAST_UNITS = 1
 
 UNITS = (
     [(2, 0, 128, 2, 2048, 256 * v, 2, 0) for v in range(8)]
@@ -605,6 +607,11 @@
 COUNT = len(UNITS)
 
 
+def parts_of(unit):
+    late = isinstance(unit, int) and unit >= COUNT - LAST_UNITS
+    return LAST_PARTS if late else PARTS
+
+
 def stacked_heads(block, heads):
     lane = lax.broadcasted_iota(jnp.int32, block.shape, 1) // HEAD_DIM
     zero = jnp.zeros_like(block)
@@ -626,7 +633,7 @@
     part_a, part_b, part_c,
     recv_a1, recv_a2, recv_az, recv_b1, recv_b2, recv_bz, recv_cz, recv_c1, recv_c2,
     wide_v, deep_v, dkv_v, xbuf, ybuf, yfar, ydown, yout, other_v, hid_v,
-    dm_v, db_v, datt_v, x_v, c_v, grad_v, q_v, kv_v, dproj_v, bias_v, cos_v, sin_v, edge_v, far_v,
+    dm_v, x_v, c_v, grad_v, q_v, kv_v, dproj_v, bias_v, cos_v, sin_v, far_v,
     vec_sum, vec_recv, vec_z,
     send_sem, recv_sem, load_sem, far_send, far_recv, w_sem, hid_sem, hid_send, hid_recv,
     oth_send, oth_recv, q_send, q_recv, x_sem, edge_send, edge_recv, vec_send, vec_rsem, out_sem, halo_send, halo_recv,
@@ -774,53 +781,69 @@
                 pieces[z].astype(f32) + recv[0, z - 1].astype(f32) + recv[1, z].astype(f32)
             )
 
-    def hop(slot, which, index):
-        a, b, cc = part_a.at[slot], part_b.at[slot], part_c.at[slot]
+    def views(unit):
+        slot = unit % RING if isinstance(unit, int) else lax.rem(unit, RING)
+        parts = parts_of(unit)
+        a, b = pl.ds(0, parts[1]), pl.ds(0, parts[2] - parts[1])
+        return (
+            slot,
+            part_a.at[slot, :, :, :, a], recv_a1.at[slot, :, :, a], recv_a2.at[slot, :, a],
+            recv_az.at[slot, :, :, a],
+            part_b.at[slot, :, :, :, b], recv_b1.at[slot, :, :, b], recv_b2.at[slot, :, b],
+            recv_bz.at[slot, :, :, b],
+            part_c.at[slot], recv_c1.at[slot], recv_c2.at[slot], recv_cz.at[slot],
+            parts[3] > parts[2],
+        )
+
+    def hop(unit, which, index):
+        slot, a, a1, a2, _, b, b1, b2, _, cc, c1, c2, _, _ = views(unit)
         source, target, device = {
-            (0, 0): lambda: (a.at[1 - x], recv_a1.at[slot], dev_x),
-            (0, 1): lambda: (a.at[x, 1 - y], recv_a2.at[slot], dev_y),
-            (1, 0): lambda: (b.at[1 - y], recv_b1.at[slot], dev_y),
-            (1, 1): lambda: (b.at[y, 1 - x], recv_b2.at[slot], dev_x),
-            (2, 0): lambda: (cc.at[z, 1 - x], recv_c1.at[slot], dev_x),
-            (2, 1): lambda: (cc.at[z, x, 1 - y], recv_c2.at[slot], dev_y),
+            (0, 0): lambda: (a.at[1 - x], a1, dev_x),
+            (0, 1): lambda: (a.at[x, 1 - y], a2, dev_y),
+            (1, 0): lambda: (b.at[1 - y], b1, dev_y),
+            (1, 1): lambda: (b.at[y, 1 - x], b2, dev_x),
+            (2, 0): lambda: (cc.at[z, 1 - x], c1, dev_x),
+            (2, 1): lambda: (cc.at[z, x, 1 - y], c2, dev_y),
         }[which, index]()
         return remote(
             source, target, send_sem.at[slot, which, index], recv_sem.at[slot, which, index], device
         )
 
     def put(unit, which, block):
+        low, high = parts_of(unit)[which : which + 2]
         if not isinstance(unit, int):
             columns = pl.ds(pl.multiple_of(unit * 256, 256), 256)
-            out2[PARTS[which] : PARTS[which + 1], columns] = block
+            out2[low:high, columns] = block
             return
         _, _, _, _, _, offset, out, row = UNITS[unit]
-        outs[out][row + PARTS[which] : row + PARTS[which + 1], offset : offset + 256] = block
+        outs[out][row + low : row + high, offset : offset + 256] = block
 
     def stage(unit, number):
-        slot = unit % RING if isinstance(unit, int) else lax.rem(unit, RING)
-        a, b, cc = part_a.at[slot], part_b.at[slot], part_c.at[slot]
+        slot, a, a1, a2, rz_a, b, b1, b2, rz_b, cc, c1, c2, rz_c, thirds = views(unit)
         a_z, b_z = a.at[x, y], b.at[y, x]
-        rz_a, rz_b, rz_c = recv_az.at[slot], recv_bz.at[slot], recv_cz.at[slot]
         if number == 0:
-            hop(slot, 0, 0).start()
-            hop(slot, 1, 0).start()
-            z_round0(slot, 2, cc, rz_c)
+            hop(unit, 0, 0).start()
+            hop(unit, 1, 0).start()
+            if thirds:
+                z_round0(slot, 2, cc, rz_c)
         if number == 1:
-            hop(slot, 0, 0).wait_recv()
-            a[x] = a[x] + recv_a1[slot]
-            hop(slot, 0, 1).start()
-            hop(slot, 1, 0).wait_recv()
-            b[y] = b[y] + recv_b1[slot]
-            hop(slot, 1, 1).start()
-            z_round1(slot, 2, cc, rz_c)
+            hop(unit, 0, 0).wait_recv()
+            a[x] = a[x] + a1[...]
+            hop(unit, 0, 1).start()
+            hop(unit, 1, 0).wait_recv()
+            b[y] = b[y] + b1[...]
+            hop(unit, 1, 1).start()
+            if thirds:
+                z_round1(slot, 2, cc, rz_c)
         if number == 2:
-            hop(slot, 0, 1).wait_recv()
-            a[x, y] = a[x, y] + recv_a2[slot]
+            hop(unit, 0, 1).wait_recv()
+            a[x, y] = a[x, y] + a2[...]
             z_round0(slot, 0, a_z, rz_a)
-            hop(slot, 1, 1).wait_recv()
-            b[y, x] = b[y, x] + recv_b2[slot]
+            hop(unit, 1, 1).wait_recv()
+            b[y, x] = b[y, x] + b2[...]
             z_round0(slot, 1, b_z, rz_b)
-            z_round2(slot, 2, cc, rz_c)
+            if thirds:
+                z_round2(slot, 2, cc, rz_c)
         if number == 3:
             z_round1(slot, 0, a_z, rz_a)
             z_round1(slot, 1, b_z, rz_b)
@@ -828,19 +851,22 @@
             def keep(value):
                 cc[z] = value.astype(bf)
 
-            z_final(slot, 2, cc, rz_c, keep)
-            hop(slot, 2, 0).start()
+            if thirds:
+                z_final(slot, 2, cc, rz_c, keep)
+                hop(unit, 2, 0).start()
         if number == 4:
             z_round2(slot, 0, a_z, rz_a)
             z_round2(slot, 1, b_z, rz_b)
-            hop(slot, 2, 0).wait_recv()
-            cc[z, x] = cc[z, x] + recv_c1[slot]
-            hop(slot, 2, 1).start()
+            if thirds:
+                hop(unit, 2, 0).wait_recv()
+                cc[z, x] = cc[z, x] + c1[...]
+                hop(unit, 2, 1).start()
         if number == 5:
             z_final(slot, 0, a_z, rz_a, functools.partial(put, unit, 0))
             z_final(slot, 1, b_z, rz_b, functools.partial(put, unit, 1))
-            hop(slot, 2, 1).wait_recv()
-            put(unit, 2, cc[z, x, y].astype(f32) + recv_c2[slot].astype(f32))
+            if thirds:
+                hop(unit, 2, 1).wait_recv()
+                put(unit, 2, cc[z, x, y].astype(f32) + c2[...].astype(f32))
 
     def sums(step):
         for number in range(1, 6):
@@ -855,17 +881,11 @@
                     stage(unit, number)
 
     def sent(unit):
-        slot = unit % RING
-        for which in range(3):
+        slot, a, _, _, rz_a, b, _, _, rz_b, cc, _, _, rz_c, thirds = views(unit)
+        whole = [(a.at[x, y], rz_a), (b.at[y, x], rz_b)] + ([(cc, rz_c)] if thirds else [])
+        for which, (pieces, recv) in enumerate(whole):
             for index in range(2):
-                hop(slot, which, index).wait_send()
-        for which, (pieces, recv) in enumerate(
-            (
-                (part_a.at[slot, x, y], recv_az.at[slot]),
-                (part_b.at[slot, y, x], recv_bz.at[slot]),
-                (part_c.at[slot], recv_cz.at[slot]),
-            )
-        ):
+                hop(unit, which, index).wait_send()
 
             @pl.when(is_end)
             def _():
@@ -876,7 +896,9 @@
                 z_send(slot, which, pieces, recv, 1).wait_send()
                 z_send(slot, which, pieces, recv, 2).wait_send()
 
-    def multiply(slot, xslot, own, far):
+    def multiply(unit, xslot, own, far):
+        slot, parts = views(unit)[0], parts_of(unit)
+
         def step(i, carry):
             columns = pl.ds(pl.multiple_of(i * 512, 512), 512)
             for xi in range(2):
@@ -887,9 +909,10 @@
                 for k in range(4):
                     zi, yi = 2 * i + k // 2, k % 2
                     block = total[k * 128 : k * 128 + 128]
-                    part_a[slot, xi, yi, zi] = block[PARTS[0] : PARTS[1]]
-                    part_b[slot, yi, xi, zi] = block[PARTS[1] : PARTS[2]]
-                    part_c[slot, zi, xi, yi] = block[PARTS[2] : PARTS[3]]
+                    part_a[slot, xi, yi, zi, : parts[1]] = block[: parts[1]]
+                    part_b[slot, yi, xi, zi, : parts[2] - parts[1]] = block[parts[1] : parts[2]]
+                    if parts[3] > parts[2]:
+                        part_c[slot, zi, xi, yi] = block[parts[2] :]
             return carry
 
         lax.fori_loop(0, 2, step, 0)
@@ -907,7 +930,7 @@
         far_copy(pair_columns(dm_v, 256, 0, 1 - c, xi), ydown.at[xi], 3 + xi) for xi in range(2)
     ]
     far_db = [
-        far_copy(pair_columns(db_v, 256, 0, 1 - c, xi), yout.at[xi], 5 + xi) for xi in range(2)
+        far_copy(other_v.at[xi, 1 - c], yout.at[xi], 5 + xi) for xi in range(2)
     ]
     far_dq = [
         remote(
@@ -1135,11 +1158,11 @@
         def _():
             far_n2.wait_recv()
 
-        gate_unit(step)
-
         @pl.when(step >= BEHIND)
         def _():
             sums(step - BEHIND)
+
+        gate_unit(step)
 
         return carry
 
@@ -1188,12 +1211,15 @@
         _, _, _, right, width, offset, _, _ = UNITS[unit]
         if unit >= RING:
             sent(unit - RING)
-        slot, xslot = unit % RING, {8: 1, 9: 0, 10: 1, 11: 0, 12: 1}.get(unit, 0)
-        own = {3: dm_v, 1: db_v, 0: dproj_v}[right]
+        xslot = {8: 1, 9: 0, 10: 1, 11: 0, 12: 1}.get(unit, 0)
+        if right == 1:
+            own = lambda xi: other_v[xi, c]
+        else:
+            own = lambda xi: pair_columns({3: dm_v, 0: dproj_v}[right], width, offset, c, xi)[...]
         far = {3: ydown, 1: yout}.get(right, yfar.at[max(unit - 13, 0)])
         multiply(
-            slot, xslot,
-            lambda xi: pair_columns(own, width, offset, c, xi)[...],
+            unit, xslot,
+            own,
             lambda xi: far[xi],
         )
         stage(unit, 0)
@@ -1231,7 +1257,9 @@
         dmid = cot + norm_backward(dn, hat, inverse, gain2_ref[...])
         vec_sum[0, 2:3] += jnp.sum(dmid * branch, 0, keepdims=True)
         grad_v[at, :] = dmid
-        db_v[at, :] = (dmid * scale_attn_ref[...]).astype(bf)
+        branch_grad = (dmid * scale_attn_ref[...]).astype(bf)
+        for k in range(4):
+            other_v[k // 2, k % 2, at, :] = branch_grad[:, 256 * k : 256 * k + 256]
         return carry
 
     out_copy = local_copy(c_v, out_hbm, out_sem.at[0])
@@ -1246,8 +1274,13 @@
     def attended_grads():
         for k in range(2):
             wo_copies[k].wait()
+        out_copy.wait()
         for k in range(2):
-            datt_v[:, 512 * k : 512 * k + 512] = contract_back(db_v[...], deep_v[k]).astype(bf)
+            total = None
+            for j in range(4):
+                term = contract_back(other_v[j // 2, j % 2], deep_v[k, :, 256 * j : 256 * j + 256])
+                total = term if total is None else total + term
+            c_v[:, 512 * k : 512 * k + 512] = total.astype(bf)
         for copy in far_db:
             copy.wait_recv()
 
@@ -1259,7 +1292,7 @@
                 own = slice(block * 128, block * 128 + 128)
                 window = slice(block * 128, block * 128 + 256)
                 queries = stacked_heads(q_v[own, lanes] * 0.125, heads)
-                grads = stacked_heads(datt_v[own, lanes], heads)
+                grads = stacked_heads(c_v[own, lanes], heads)
                 keys = kv_v[0, window, lanes]
                 bias = jnp.concatenate([bias_v[block]] * (heads // 2), 1)
                 scores = contract_back(keys, queries) + bias
@@ -1294,15 +1327,18 @@
         lax.fori_loop(0, D // lanes_of, step, 0)
 
     to_left = remote(
-        edge_v.at[0], far_v.at[1], edge_send.at[0], edge_recv.at[0], (dp, seq - 1)
+        hid_v.at[0, pl.ds(0, 256)], far_v.at[1], edge_send.at[0], edge_recv.at[0], (dp, seq - 1)
     )
     to_right = remote(
-        edge_v.at[1], far_v.at[0], edge_send.at[1], edge_recv.at[1], (dp, seq + 1)
+        hid_v.at[1, pl.ds(0, 256)], far_v.at[0], edge_send.at[1], edge_recv.at[1], (dp, seq + 1)
     )
 
     def edges_out():
-        edge_v[0] = dkv_v[:, 0:HALF].astype(bf)
-        edge_v[1] = dkv_v[:, HALF + TOK :].astype(bf)
+        for side, first in ((0, 0), (1, HALF + TOK)):
+            for k in range(4):
+                hid_v[side, 64 * k : 64 * k + 64] = dkv_v[
+                    k // 2, first : first + HALF, 512 * (k % 2) : 512 * (k % 2) + 512
+                ].astype(bf)
 
         @pl.when(has_left)
         def _():
@@ -1316,12 +1352,18 @@
         @pl.when(has_left)
         def _():
             to_right.wait_recv()
-            dkv_v[:, HALF : 2 * HALF] += far_v[0].astype(f32)
+            for k in range(4):
+                dkv_v[k // 2, HALF : 2 * HALF, 512 * (k % 2) : 512 * (k % 2) + 512] += far_v[
+                    0, 64 * k : 64 * k + 64
+                ].astype(f32)
 
         @pl.when(has_right)
         def _():
             to_left.wait_recv()
-            dkv_v[:, TOK : TOK + HALF] += far_v[1].astype(f32)
+            for k in range(4):
+                dkv_v[k // 2, TOK : TOK + HALF, 512 * (k % 2) : 512 * (k % 2) + 512] += far_v[
+                    1, 64 * k : 64 * k + 64
+                ].astype(f32)
 
         for k in range(D // 128):
             lanes = slice(k * 128, k * 128 + 128)
@@ -1431,14 +1473,12 @@
         halo_right.wait_send()
         to_right.wait_send()
 
-    out_copy.wait()
     grad_copy.wait()
 
 
-BEHIND = 4
+BEHIND = 2
 ORDER = (
-    "S4 P8 E S5 P9 D S6 P10 A0 O S7 P11 A1 I S8 P12 W0 S9 W1 Q P13 N S10 V0 P14 S11 V1 P15 S12 V2"
-    " S13 V3 S14 V4 S15 S16 S17 S18 S19"
+    "P8 P9 E S6 P10 D A0 O S7 P11 A1 S8 P12 I Q S9 P13 W0 S10 P14 W1 N S11 P15 V0 S12 V1 S13 V2 S14 V3 S15 V4 S16 S17 S18 S19"
 )
 
 
@@ -1450,7 +1490,7 @@
     vmem = pl.BlockSpec(memory_space=pltpu.VMEM)
     smem = pl.BlockSpec(memory_space=pltpu.SMEM)
     shape = jax.ShapeDtypeStruct
-    size = (PARTS[1], PARTS[2] - PARTS[1], PARTS[3] - PARTS[2])
+    size = (LAST_PARTS[1], LAST_PARTS[2] - LAST_PARTS[1], PARTS[3] - PARTS[2])
     dma = pltpu.SemaphoreType.DMA
     ext = TOK + 2 * HALF
     scratch = [
@@ -1479,8 +1519,6 @@
         pltpu.VMEM((TOK, D), bf),
         pltpu.VMEM((TOK, D), bf),
         pltpu.VMEM((TOK, D), bf),
-        pltpu.VMEM((TOK, D), bf),
-        pltpu.VMEM((TOK, D), bf),
         pltpu.VMEM((TOK, D), f32),
         pltpu.VMEM((TOK, D), bf),
         pltpu.VMEM((2, ext, D), bf),
@@ -1488,8 +1526,7 @@
         pltpu.VMEM((TOK // 128, 256, 256), f32),
         pltpu.VMEM((TOK, 128), f32),
         pltpu.VMEM((TOK, 128), f32),
-        pltpu.VMEM((2, 2, HALF, D), bf),
-        pltpu.VMEM((2, 2, HALF, D), bf),
+        pltpu.VMEM((2, 256, 512), bf),
         pltpu.VMEM((4, 8, D), f32),
         pltpu.VMEM((3, 8, D), f32),
         pltpu.VMEM((4, 8, D), f32),

time: 180 us -> 171 us (0.950)
  Pallas kernels: 179 us -> 170 us
    pallas_call x1, Pallas kernels: 174 us -> 165 us  [layer(): pl.pallas_call(layer_kernel, out_shape=[shape((TOK, D), bf), shape((TOK,...]
where the time goes in v2:
time: 171 us
  Pallas kernels  170 us (99%)
    pallas_call x1, Pallas kernels, layer(): pl.pallas_call(layer_kernel, out_shape=[shape((TOK, D), bf), shape((TOK,...  165 us
    pallas_call x1, Pallas kernels, layer(): pl.pallas_call(finish_kernel, out_shape=[shape(v.shape, v.dtype) for v in...  5.4 us

profile of v2, /device:TPU:0, one launch (start us, length us, event | category | flops | bytes accessed | tf_op | source)
XLA Modules:
  0.0 170.8 jit_solution(8070590641123231154)
XLA Ops:
  0.6 164.6 %layer.1 = (bf16[512,1024]{1,0:T(8,128)(2,1)}, f32[512,1024]{1,0:T(8,128)}, f32[128,768]{1,0:T(8,128)}, f32[128,256]{1,0:T(8,128)}, f32[128,2048]{1,0:T(8,128)},...) custom-call(s32[1,3]{1,0:T(1,128)} %clip_ref.1, ...), custom_call_target="tpu_custom_call" | custom-call | tf_op jit(solution)/shard_map/layer/pallas_call | solution.py:1555
  165.2 5.4 %finish.1 = (bf16[512,1024]{1,0:T(8,128)(2,1)}, f32[512,1024]{1,0:T(8,128)}, f32[128,768]{1,0:T(8,128)}, f32[128,256]{1,0:T(8,128)}, f32[128,2048]{1,0:T(8,128)}...) custom-call(bf16[512,1024]{1,0:T(8,128)(2,1)} %get-tuple-element.31., ...), custom_call_target="tpu_custom_call" | custom-call | tf_op jit(solution)/shard_map/finish/pallas_call | solution.py:1581

commit v3 on v2

--- a/solution.py
+++ b/solution.py
@@ -1448,7 +1448,7 @@
         "N": norm_one_back,
         "Q": far_dq_wait,
     }
-    for word in ORDER.split():
+    for word in " ".join(ORDER).split():
         if word in actions:
             actions[word]()
         elif word[0] == "P":
@@ -1478,7 +1478,16 @@
 
 BEHIND = 2
 ORDER = (
-    "P8 P9 E S6 P10 D A0 O S7 P11 A1 S8 P12 I Q S9 P13 W0 S10 P14 W1 N S11 P15 V0 S12 V1 S13 V2 S14 V3 S15 V4 S16 S17 S18 S19"
+    "P8 P9 E S6",
+    "P10 D A0 O",
+    "S7 P11 A1 S8",
+    "P12 I Q S9",
+    "P13 W0 S10 P14",
+    "W1 N S11 P15",
+    "V0 S12 V1 S13",
+    "V2 S14 V3 S15",
+    "V4 S16 S17 S18",
+    "S19",
 )
 
 

time: 171 us -> 171 us (level)
  no operation moved by 1% of the time
where the time goes in v3:
time: 171 us
  Pallas kernels  170 us (99%)
    pallas_call x1, Pallas kernels, layer(): pl.pallas_call(layer_kernel, out_shape=[shape((TOK, D), bf), shape((TOK,...  165 us
    pallas_call x1, Pallas kernels, layer(): pl.pallas_call(finish_kernel, out_shape=[shape(v.shape, v.dtype) for v in...  5.4 us

profile of v3, /device:TPU:0, one launch (start us, length us, event | category | flops | bytes accessed | tf_op | source)
XLA Modules:
  0.0 170.8 jit_solution(8070590641123231154)
XLA Ops:
  0.6 164.6 %layer.1 = (bf16[512,1024]{1,0:T(8,128)(2,1)}, f32[512,1024]{1,0:T(8,128)}, f32[128,768]{1,0:T(8,128)}, f32[128,256]{1,0:T(8,128)}, f32[128,2048]{1,0:T(8,128)},...) custom-call(s32[1,3]{1,0:T(1,128)} %clip_ref.1, ...), custom_call_target="tpu_custom_call" | custom-call | tf_op jit(solution)/shard_map/layer/pallas_call | solution.py:1564
  165.2 5.4 %finish.1 = (bf16[512,1024]{1,0:T(8,128)(2,1)}, f32[512,1024]{1,0:T(8,128)}, f32[128,768]{1,0:T(8,128)}, f32[128,256]{1,0:T(8,128)}, f32[128,2048]{1,0:T(8,128)}...) custom-call(bf16[512,1024]{1,0:T(8,128)(2,1)} %get-tuple-element.31., ...), custom_call_target="tpu_custom_call" | custom-call | tf_op jit(solution)/shard_map/finish/pallas_call | solution.py:1590

commit v4 on v3

--- a/solution.py
+++ b/solution.py
@@ -1592,7 +1592,7 @@
         out_shape=[shape(v.shape, v.dtype) for v in results[:6]] + [shape((1, D), f32)] * 6,
         in_specs=[hbm] * 6 + [vmem],
         out_specs=[hbm] * 6 + [vmem] * 6,
-        scratch_shapes=[pltpu.VMEM(v.shape, v.dtype) for v in results[:6]] + [dma((2, 6))],
+        scratch_shapes=[pltpu.VMEM(v.shape, v.dtype) for v in results[:6]] + [dma((2, 24))],
         compiler_params=pltpu.CompilerParams(vmem_limit_bytes=64 * 2**20 - 2**16),
         name="finish",
     )(*results)
@@ -1601,14 +1601,17 @@
 
 def finish_kernel(*refs):
     sources, targets, held, sems = refs[:6], refs[7:13], refs[19:25], refs[25]
-    arrivals = [
-        pltpu.make_async_copy(source, target, sems.at[0, k])
-        for k, (source, target) in enumerate(zip(sources, held))
-    ]
-    departures = [
-        pltpu.make_async_copy(source, target, sems.at[1, k])
-        for k, (source, target) in enumerate(zip(held, targets))
-    ]
+    arrivals, departures = [], []
+    for k, (source, middle, target) in enumerate(zip(sources, held, targets)):
+        size = source.shape[0] // 4
+        for n in range(4):
+            rows = pl.ds(n * size, size)
+            arrivals.append(
+                pltpu.make_async_copy(source.at[rows], middle.at[rows], sems.at[0, 4 * k + n])
+            )
+            departures.append(
+                pltpu.make_async_copy(middle.at[rows], target.at[rows], sems.at[1, 4 * k + n])
+            )
     for copy in arrivals:
         copy.start()
     for k in range(6):

time: 171 us -> 172 us (level)
  no operation moved by 1% of the time
where the time goes in v4:
time: 172 us
  Pallas kernels  171 us (99%)
    pallas_call x1, Pallas kernels, layer(): pl.pallas_call(layer_kernel, out_shape=[shape((TOK, D), bf), shape((TOK,...  165 us
    pallas_call x1, Pallas kernels, layer(): pl.pallas_call(finish_kernel, out_shape=[shape(v.shape, v.dtype) for v in...  6.41 us

profile of v4, /device:TPU:0, one launch (start us, length us, event | category | flops | bytes accessed | tf_op | source)
XLA Modules:
  0.0 171.8 jit_solution(15204893523835873694)
XLA Ops:
  0.6 164.6 %layer.1 = (bf16[512,1024]{1,0:T(8,128)(2,1)}, f32[512,1024]{1,0:T(8,128)}, f32[128,768]{1,0:T(8,128)}, f32[128,256]{1,0:T(8,128)}, f32[128,2048]{1,0:T(8,128)},...) custom-call(s32[1,3]{1,0:T(1,128)} %clip_ref.1, ...), custom_call_target="tpu_custom_call" | custom-call | tf_op jit(solution)/shard_map/layer/pallas_call | solution.py:1564
  165.2 6.4 %finish.1 = (bf16[512,1024]{1,0:T(8,128)(2,1)}, f32[512,1024]{1,0:T(8,128)}, f32[128,768]{1,0:T(8,128)}, f32[128,256]{1,0:T(8,128)}, f32[128,2048]{1,0:T(8,128)}...) custom-call(bf16[512,1024]{1,0:T(8,128)(2,1)} %get-tuple-element.31., ...), custom_call_target="tpu_custom_call" | custom-call | tf_op jit(solution)/shard_map/finish/pallas_call | solution.py:1590
